TPU v7x, 256 devices: a whole 4x4x8 slice. The times are simulated.
256 devices in a mesh: head: 4 (over z_lo), ctx: 64 (over z_hi, y, x, core).
Axes of the slice: x: 4, y: 4, z: 8 (z_hi: 2, z_lo: 4; z = z_hi * 4 + z_lo), core: 2. Of those that a mesh axis runs over, the one named last changes fastest.
Arguments:
- queries: bfloat16 [64, 256, 4096], P('ctx', 'head'), may hold values from -6 to 6
- key_state_rows: bfloat16 [64, 256, 512], P('ctx', 'head'), may hold values from -6 to 6
- value_state_rows: bfloat16 [64, 256, 512], P('ctx', 'head'), may hold values from -6 to 6
- output_state_rows: bfloat16 [64, 256, 4096], P('ctx', 'head'), may hold values from -6 to 6
- output_gradient: bfloat16 [64, 256, 4096], P('ctx', 'head'), may hold values from -0.5390625 to 0.5390625
- logsumexp_rows: float32 [64, 256, 32], P('ctx', None, 'head'), may hold values from 2 to 4
- doc_lengths: int32 [64], replicated, may hold values from 1 to 1024, 16384 in all
Outputs:
- query_grad: bfloat16 [64, 256, 4096], P('ctx', 'head')
- gradient_keys: bfloat16 [64, 256, 512], P('ctx', 'head')
- gradient_values: bfloat16 [64, 256, 512], P('ctx', 'head')
Inputs may be any that keep to these rules, and one draw needn't show every extreme that they name: `doc_lengths`: the 64 lengths sum to 16384; the longest is exactly 1024.
All inputs are finite; a program needn't handle non-finite values.
Results may differ from a plain program's by a relative error of at most 0.0049.
Values may be sent and summed in bfloat16 or wider, within the bound.
A program may use at most 64 MiB of HBM per device.

v0:
```python
import jax
import jax.numpy as jnp
from jax import lax
from jax.experimental import pallas as pl
from jax.experimental.pallas import tpu as pltpu
from jax.sharding import PartitionSpec as P

MESH = pl.DeviceIdType.MESH
F32 = jnp.float32
BF16 = jnp.bfloat16
SCALE = 128 ** (-0.5)
GROUPS = 16


def kernel(
    q_ref, k_ref, v_ref, o_ref, do_ref, lse_ref, len_ref,
    dq_ref, dk_ref, dv_ref,
    kvs, kvb, qb, dob, lsec, lset, lseb, dls, dlb, acc, dqt, dqs, dqr, pxs, pxr, rts, ret,
    s_kv, s_kvn, r_kv, s_kvp, r_kvp, s_q, r_q, s_do, r_do,
    s_l, r_l, s_d, r_d, s_dq, r_dq, s_px, r_px, s_rt, s_rtp, r_rt, r_rtn,
):
    z = lax.axis_index("head")
    c = lax.axis_index("ctx")
    pair = c // 4
    own = c % 4
    xq = own // 2
    core = c % 2
    zb = z % 2
    zp = z // 2
    g = 2 * xq + zb
    first = pair == 0
    last = pair == GROUPS - 1

    def zx(e):
        return (z, z + 1 - 2 * zb, (z + 2) % 4, 3 - z)[e]

    def xx(a):
        return xq if a == 0 else 1 - xq

    def kx(b):
        return core if b == 0 else 1 - core

    def at(off, a, b):
        return 4 * (pair + off) + 2 * xx(a) + kx(b)

    def remote(src, dst, ssem, rsem, dev):
        return pltpu.make_async_remote_copy(
            src_ref=src, dst_ref=dst, send_sem=ssem, recv_sem=rsem,
            device_id=dev, device_id_type=MESH,
        )

    def await_bytes(ref, sem):
        pltpu.make_async_copy(ref, ref, sem).wait()

    barrier = pltpu.get_barrier_semaphore()
    for a in range(2):
        for b in range(2):
            for e in range(4):
                if a or b or e:
                    pl.semaphore_signal(barrier, inc=1, device_id=(zx(e), at(0, a, b)), device_id_type=MESH)

    @pl.when(jnp.logical_not(first))
    def _():
        for a in range(2):
            for e in range(4):
                pl.semaphore_signal(barrier, inc=1, device_id=(zx(e), at(-1, a, 0)), device_id_type=MESH)

    @pl.when(jnp.logical_not(last))
    def _():
        for a in range(2):
            for e in range(4):
                pl.semaphore_signal(barrier, inc=1, device_id=(zx(e), at(1, a, 0)), device_id_type=MESH)

    for n in range(4):
        kvs[:, n * 256 : n * 256 + 128] = k_ref[0, :, n * 128 : (n + 1) * 128]
        kvs[:, n * 256 + 128 : (n + 1) * 256] = v_ref[0, :, n * 128 : (n + 1) * 128]

    pl.semaphore_wait(barrier, 15 + 8 * ((pair + GROUPS - 1) // GROUPS) + 8 * ((2 * GROUPS - 2 - pair) // GROUPS))

    def send_kv(off):
        slot = 4 * (1 - off) + own
        for a in range(2):
            for e in range(4):
                there = 2 * xx(a) + zx(e) % 2
                src = kvs.at[:, pl.ds(pl.multiple_of(there * 256, 256), 256)]
                dst = kvb.at[pl.ds(pl.multiple_of(slot * 256 + z * 64, 64), 64)]
                if off == 0 and a == 0 and e == 0:
                    pltpu.make_async_copy(src, dst, r_kv.at[slot]).start()
                else:
                    remote(src, dst, s_kvn if off else s_kv, r_kv.at[slot], (zx(e), at(off, a, 0))).start()

    send_kv(0)

    @pl.when(jnp.logical_not(last))
    def _():
        send_kv(1)

    rows_own = pl.ds(pl.multiple_of(own * 128 + zb * 64, 64), 64)
    for a in range(2):
        for b in range(2):
            for e in range(2):
                lane = (2 * xx(a) + zx(e) % 2) * 1024 + kx(b) * 512
                cols = pl.ds(pl.multiple_of(lane, 512), 512)
                for ref, buf, ss, rr in ((q_ref, qb, s_q, r_q), (do_ref, dob, s_do, r_do)):
                    src = ref.at[0, :, cols]
                    dst = buf.at[rows_own]
                    if a or b or e:
                        remote(src, dst, ss, rr.at[own], (zx(e), at(0, a, b))).start()
                    else:
                        pltpu.make_async_copy(src, dst, rr.at[own]).start()

    lsec[...] = jnp.zeros_like(lsec)
    lsec[:, 0:8] = lse_ref[0]
    turned = lsec[...].T
    for p in range(2):
        lset[p] = turned[0:8, p * 128 : (p + 1) * 128]
    to_x = z // 2
    for e in (0, 2):
        half = zx(e) // 2
        for b in range(2):
            dev = (zx(e), 4 * pair + 2 * to_x + kx(b))
            src, dst = lset.at[half], lseb.at[own]
            if e == 0 and b == 0:
                @pl.when(to_x == xq)
                def _():
                    pltpu.make_async_copy(src, dst, r_l.at[own]).start()

                @pl.when(to_x != xq)
                def _():
                    remote(src, dst, s_l.at[0], r_l.at[own], dev).start()
            else:
                remote(src, dst, s_l.at[e + b], r_l.at[own], dev).start()

    lanes = lax.broadcasted_iota(jnp.int32, (64, 128), 1)
    delta = jnp.zeros((64, 128), F32)
    for n in range(32):
        part = do_ref[0, :, n * 128 : (n + 1) * 128].astype(F32) * o_ref[0, :, n * 128 : (n + 1) * 128].astype(F32)
        delta = jnp.where(lanes == n, jnp.sum(part, axis=1, keepdims=True), delta)
    both = jnp.concatenate([delta, delta], axis=0).T
    for n in range(4):
        dls[n] = both[n * 8 : (n + 1) * 8]
    for a in range(2):
        for b in range(2):
            for e in range(2):
                src = dls.at[2 * xx(a) + zx(e) % 2]
                dst = dlb.at[pl.ds(pl.multiple_of(own * 16 + zb * 8, 8), 8)]
                if a or b or e:
                    remote(src, dst, s_d, r_d.at[own], (zx(e), at(0, a, b))).start()
                else:
                    pltpu.make_async_copy(src, dst, r_d.at[own]).start()

    place = lax.broadcasted_iota(jnp.int32, (8, 128), 1) + (pair * 1024 + zp * 128)

    def seek(d, carry):
        begin, found = carry
        found = tuple(jnp.where(place + 256 * n >= begin, begin, f) for n, f in enumerate(found))
        return begin + len_ref[d], found

    _, opens = lax.fori_loop(0, 64, seek, (jnp.int32(0), tuple(jnp.zeros((8, 128), jnp.int32) for _ in range(4))))
    for n in range(4):
        dqt[n] = jnp.zeros((128, 512), F32)
    acc[...] = jnp.zeros_like(acc)

    @pl.when(first)
    def _():
        kvb[0:1024] = jnp.zeros((1024, 256), BF16)

    def blk(b):
        return pl.ds(pl.multiple_of(b * 256, 256), 256)

    partner = (z, at(0, 0, 1))
    for i in range(4):
        b = 2 * i + core

        def hand_on():
            await_bytes(kvb.at[blk(b)], r_kv.at[b])
            remote(kvb.at[blk(b)], kvb.at[blk(b)], s_kvp, r_kvp.at[b], partner).start()

        if i < 2:
            pl.when(jnp.logical_not(first))(hand_on)
        else:
            hand_on()
    for i in range(4):
        b = 2 * i + 1 - core

        def take():
            await_bytes(kvb.at[blk(b)], r_kvp.at[b])

        if i < 2:
            pl.when(jnp.logical_not(first))(take)
        else:
            take()

    for n in range(4):
        await_bytes(lseb.at[n], r_l.at[n])
        await_bytes(dlb.at[n * 16 : n * 16 + 16], r_d.at[n])
        await_bytes(qb.at[n * 128 : n * 128 + 128], r_q.at[n])
        await_bytes(dob.at[n * 128 : n * 128 + 128], r_do.at[n])
    steps = lax.broadcasted_iota(jnp.int32, (256, 128), 0)
    low = lax.broadcasted_iota(jnp.int32, (8, 128), 1) < 64

    def piece(j):
        bx = (xq + j // 2) % 2
        bk = (core + j % 2) % 2
        bi = 2 * bx + bk
        mine = pl.ds(pl.multiple_of(bi * 128, 128), 128)
        deltas = dlb.at[pl.ds(pl.multiple_of(bi * 16, 16), 16)]
        lse_all = lseb[bi]
        delta_all = jnp.where(low, deltas[0:8], deltas[8:16])
        lse_mine = jnp.where(core == 0, lse_all[0:4], lse_all[4:8])
        delta_mine = jnp.where(core == 0, delta_all[0:4], delta_all[4:8])
        lse_row = jnp.concatenate([lse_mine[n : n + 1] for n in range(4)], axis=1)
        delta_row = jnp.concatenate([delta_mine[n : n + 1] for n in range(4)], axis=1)
        where_open = jnp.where(bi == 0, opens[0], jnp.where(bi == 1, opens[1], jnp.where(bi == 2, opens[2], opens[3])))[0:1]
        where_here = (place + 256 * bi)[0:1]
        qp = qb[mine]
        dop = dob[mine]
        qm = jnp.concatenate([qp[:, n * 128 : (n + 1) * 128] for n in range(4)], axis=0)
        dom = jnp.concatenate([dop[:, n * 128 : (n + 1) * 128] for n in range(4)], axis=0)

        def lag(l, _):
            b = bi + l
            rows = blk(b)
            key = kvb[rows, 0:128]
            value = kvb[rows, 128:256]
            base = (4 * pair - 4 + b) * 256
            allowed = (steps >= where_open - base) & (steps <= where_here - base)
            allowed = jnp.concatenate([allowed] * 4, axis=1)
            scores = lax.dot_general(key, qm, (((1,), (1,)), ((), ())), preferred_element_type=F32)
            weights = jnp.where(allowed, jnp.exp(scores * SCALE - lse_row), 0.0)
            grads = lax.dot_general(value, dom, (((1,), (1,)), ((), ())), preferred_element_type=F32)
            shifted = (weights * (grads - delta_row) * SCALE).astype(BF16)
            acc[rows, 128:256] += jnp.dot(weights.astype(BF16), dom, preferred_element_type=F32)
            acc[rows, 0:128] += jnp.dot(shifted, qm, preferred_element_type=F32)
            dqt[bi] += lax.dot_general(key, shifted, (((0,), (0,)), ((), ())), preferred_element_type=F32)
            return 0

        lax.fori_loop(0, 5, lag, 0)
        done = dqt[bi]
        for n in range(4):
            dqs[j * 128 : (j + 1) * 128, n * 128 : (n + 1) * 128] = done[:, n * 128 : (n + 1) * 128].T.astype(BF16)
    slot = 2 * g + core
    for j in range(4):
        piece(j)
    for j in range(4):
        bx = (xq + j // 2) % 2
        bk = (core + j % 2) % 2
        bi = 2 * bx + bk
        for e in range(2):
            src = dqs.at[pl.ds(pl.multiple_of(j * 128 + (zx(e) % 2) * 64, 64), 64)]
            dst = dqr.at[slot]
            if e:
                remote(src, dst, s_dq, r_dq, (zx(1), 4 * pair + bi)).start()
            elif j:
                remote(src, dst, s_dq, r_dq, (z, 4 * pair + bi)).start()
            else:
                pltpu.make_async_copy(src, dst, r_dq).start()

    for i in range(4):
        pxs[i] = acc[blk(2 * i + 1 - core)].astype(BF16)
        remote(pxs.at[i], pxr.at[i], s_px, r_px.at[i], partner).start()

    def send_back(off):
        for a in range(2):
            i = (2 * (1 - off)) + xx(a)
            for e in range(4):
                src = rts.at[i, pl.ds(pl.multiple_of(zx(e) * 64, 64), 64)]
                dst = ret.at[off * 8 + z * 2 + xq]
                if off == 0 and a == 0 and e == 0:
                    pltpu.make_async_copy(src, dst, r_rt).start()
                else:
                    remote(src, dst, s_rtp if off else s_rt, r_rtn if off else r_rt, (zx(e), at(-off, a, 0))).start()

    for i in range(2):
        await_bytes(pxr.at[i], r_px.at[i])
        rts[i] = (acc[blk(2 * i + core)] + pxr[i].astype(F32)).astype(BF16)

    @pl.when(jnp.logical_not(first))
    def _():
        send_back(1)

    for i in range(2, 4):
        await_bytes(pxr.at[i], r_px.at[i])
        rts[i] = (acc[blk(2 * i + core)] + pxr[i].astype(F32)).astype(BF16)
    send_back(0)

    await_bytes(ret.at[0:8], r_rt)

    @pl.when(last)
    def _():
        ret[8:16] = jnp.zeros((8, 64, 256), BF16)

    @pl.when(jnp.logical_not(last))
    def _():
        await_bytes(ret.at[8:16], r_rtn)

    for n in range(4):
        total = jnp.zeros((64, 256), F32)
        for off in range(2):
            for p in range(2):
                total = total + ret[off * 8 + (2 * p + n % 2) * 2 + n // 2].astype(F32)
        dk_ref[0, :, n * 128 : (n + 1) * 128] = total[:, 0:128].astype(BF16)
        dv_ref[0, :, n * 128 : (n + 1) * 128] = total[:, 128:256].astype(BF16)

    await_bytes(dqr, r_dq)
    for n in range(8):
        dq_ref[0, :, n * 512 : (n + 1) * 512] = dqr[n]

    await_bytes(kvb.at[0 : 7 * 64], s_kv)
    await_bytes(qb.at[0 : 7 * 64], s_q)
    await_bytes(dob.at[0 : 7 * 64], s_do)
    await_bytes(dqs.at[0 : 7 * 64], s_dq)
    await_bytes(pxs, s_px)
    await_bytes(ret.at[0:7], s_rt)
    await_bytes(dlb.at[0 : 7 * 8], s_d)
    for n in range(1, 4):
        await_bytes(lset.at[0], s_l.at[n])

    @pl.when(to_x != xq)
    def _():
        await_bytes(lset.at[0], s_l.at[0])

    @pl.when(jnp.logical_not(last))
    def _():
        await_bytes(kvb.at[0:512], s_kvn)

    @pl.when(first)
    def _():
        await_bytes(kvb.at[0:512], s_kvp)

    @pl.when(jnp.logical_not(first))
    def _():
        await_bytes(kvb.at[0:1024], s_kvp)
        await_bytes(ret.at[0:8], s_rtp)


def local(queries, keys, values, outputs, gradient, sums, lengths):
    vmem = pl.BlockSpec(memory_space=pltpu.VMEM)
    dma = pltpu.SemaphoreType.DMA
    return pl.pallas_call(
        kernel,
        out_shape=(
            jax.ShapeDtypeStruct((1, 64, 4096), BF16),
            jax.ShapeDtypeStruct((1, 64, 512), BF16),
            jax.ShapeDtypeStruct((1, 64, 512), BF16),
        ),
        in_specs=[vmem] * 6 + [pl.BlockSpec(memory_space=pltpu.SMEM)],
        out_specs=(vmem, vmem, vmem),
        scratch_shapes=[
            pltpu.VMEM((64, 1024), BF16),
            pltpu.VMEM((2048, 256), BF16),
            pltpu.VMEM((512, 512), BF16),
            pltpu.VMEM((512, 512), BF16),
            pltpu.VMEM((256, 128), F32),
            pltpu.VMEM((2, 8, 128), F32),
            pltpu.VMEM((4, 8, 128), F32),
            pltpu.VMEM((4, 8, 128), F32),
            pltpu.VMEM((64, 128), F32),
            pltpu.VMEM((2048, 256), F32),
            pltpu.VMEM((4, 128, 512), F32),
            pltpu.VMEM((512, 512), BF16),
            pltpu.VMEM((8, 64, 512), BF16),
            pltpu.VMEM((4, 256, 256), BF16),
            pltpu.VMEM((4, 256, 256), BF16),
            pltpu.VMEM((4, 256, 256), BF16),
            pltpu.VMEM((16, 64, 256), BF16),
            dma, dma, dma((8,)), dma, dma((8,)), dma, dma((4,)), dma, dma((4,)),
            dma((4,)), dma((4,)), dma, dma((4,)), dma, dma, dma, dma((4,)), dma, dma, dma, dma,
        ],
        compiler_params=pltpu.CompilerParams(
            collective_id=0, has_side_effects=True, vmem_limit_bytes=48 * 2**20
        ),
        name="attention_backward",
    )(queries, keys, values, outputs, gradient, sums, lengths)


def solution(mesh):
    in_specs = (
        P("ctx", "head", None),
        P("ctx", "head", None),
        P("ctx", "head", None),
        P("ctx", "head", None),
        P("ctx", "head", None),
        P("ctx", None, "head"),
        P(),
    )
    out_specs = (P("ctx", "head", None), P("ctx", "head", None), P("ctx", "head", None))
    return jax.shard_map(local, mesh=mesh, in_specs=in_specs, out_specs=out_specs, check_vma=False)
```

profile of v0, /device:TPU:60, one launch (start us, length us, event | category | flops | bytes accessed | tf_op | source)
XLA Modules:
  0.0 69.4 jit_solution(2861413191569823973)
XLA Ops:
  0.6 0.0 copy-start.5
  0.6 0.0 copy-start.4
  0.7 0.0 copy-start.3
  0.7 0.9 %copy.10.lse_ref = f32[1,256,8]{2,1,0:T(8,128)S(1)} copy(f32[1,256,8]{1,2,0:T(8,128)} %param.12) | data formatting | bytes 16384 | tf_op args[5]
  1.5 0.0 copy-done.5
  1.5 0.0 copy-done.4
  1.5 0.0 copy-done.3
  1.6 0.0 copy-start
  1.6 1.0 %copy-done = bf16[1,64,4096]{2,1,0:T(8,128)(2,1)S(1)} copy-done((bf16[1,64,4096]{2,1,0:T(8,128)(2,1)S(1)}, bf16[1,64,4096]{2,1,0:T(8,128)(2,1)}, u32[]{:S(2)}) %copy-start) | copy-done | bytes 524312
  2.6 0.0 copy-start.1
  2.6 1.0 %copy-done.1 = bf16[1,64,4096]{2,1,0:T(8,128)(2,1)S(1)} copy-done((bf16[1,64,4096]{2,1,0:T(8,128)(2,1)S(1)}, bf16[1,64,4096]{2,1,0:T(8,128)(2,1)}, u32[]{:S(2)}) %copy-start.1) | copy-done | bytes 524312
  3.6 0.0 copy-start.2
  3.6 1.0 %copy-done.2 = bf16[1,64,4096]{2,1,0:T(8,128)(2,1)S(1)} copy-done((bf16[1,64,4096]{2,1,0:T(8,128)(2,1)S(1)}, bf16[1,64,4096]{2,1,0:T(8,128)(2,1)}, u32[]{:S(2)}) %copy-start.2) | copy-done | bytes 524312
  4.7 62.7 %attention_backward.1 = (bf16[1,64,4096]{2,1,0:T(8,128)(2,1)S(1)}, bf16[1,64,512]{2,1,0:T(8,128)(2,1)S(1)}, bf16[1,64,512]{2,1,0:T(8,128)(2,1)S(1)}) custom-call(bf16[1,64,4096]{2,1,0:T(8,128)(2,1)S(1)} %copy-done, bf16[1,64,512]{2,1,0:T(8,128)(2,1)S(1)} %copy-done.3, bf16[1,64,512]{2,1,0:T(8,128)(2,1)S(1)} %copy-done.4, bf16[1,64,4096]{2,1,0:T(8,128)(2,1)S(1)} %copy-done.1, ...), custom_call_target="tpu_custom_call" | custom-call | tf_op jit(solution)/shard_map/attention_backward/pallas_call | solution.py:340
  67.4 0.8 %copy.14 = bf16[1,64,4096]{2,1,0:T(8,128)(2,1)} copy(bf16[1,64,4096]{2,1,0:T(8,128)(2,1)S(1)} %get-tuple-element.6) | data formatting | bytes 1048576
  68.2 0.6 copy.15
  68.8 0.6 copy.16
Async XLA Ops:
  0.6 0.9 %copy-start.5 = (s32[64]{0:T(128)S(1)}, s32[64]{0:T(128)}, u32[]{:S(2)}) copy-start(s32[64]{0:T(128)} %len_ref.1) | copy-start | bytes 772
  0.6 0.9 %copy-start.4 = (bf16[1,64,512]{2,1,0:T(8,128)(2,1)S(1)}, bf16[1,64,512]{2,1,0:T(8,128)(2,1)}, u32[]{:S(2)}) copy-start(bf16[1,64,512]{2,1,0:T(8,128)(2,1)} %v_ref.1) | copy-start | bytes 196612
  0.7 0.9 %copy-start.3 = (bf16[1,64,512]{2,1,0:T(8,128)(2,1)S(1)}, bf16[1,64,512]{2,1,0:T(8,128)(2,1)}, u32[]{:S(2)}) copy-start(bf16[1,64,512]{2,1,0:T(8,128)(2,1)} %k_ref.1) | copy-start | bytes 196612
  1.6 1.0 %copy-start = (bf16[1,64,4096]{2,1,0:T(8,128)(2,1)S(1)}, bf16[1,64,4096]{2,1,0:T(8,128)(2,1)}, u32[]{:S(2)}) copy-start(bf16[1,64,4096]{2,1,0:T(8,128)(2,1)} %q_ref.1) | copy-start | bytes 1572868
  2.6 1.0 %copy-start.1 = (bf16[1,64,4096]{2,1,0:T(8,128)(2,1)S(1)}, bf16[1,64,4096]{2,1,0:T(8,128)(2,1)}, u32[]{:S(2)}) copy-start(bf16[1,64,4096]{2,1,0:T(8,128)(2,1)} %o_ref.1) | copy-start | bytes 1572868
  3.6 1.0 %copy-start.2 = (bf16[1,64,4096]{2,1,0:T(8,128)(2,1)S(1)}, bf16[1,64,4096]{2,1,0:T(8,128)(2,1)}, u32[]{:S(2)}) copy-start(bf16[1,64,4096]{2,1,0:T(8,128)(2,1)} %do_ref.1) | copy-start | bytes 1572868
where the time goes:
time: 69.7 us; the launch traced here: 69.4 us
  Pallas kernels  62.7 us (90%)
  local copies, waits for them, and re-layouts  6.04 us (9%)
  between operations  0.71 us (1%)
    pallas_call x1, Pallas kernels, local(): pl.pallas_call(kernel, out_shape=(jax.ShapeDtypeStruct((1, 64, 4096), BF1...  62.7 us
    unnamed x16, local copies, waits for them, and re-layouts  6.04 us

commit v1 on v0

--- a/solution.py
+++ b/solution.py
@@ -15,8 +15,8 @@
 def kernel(
     q_ref, k_ref, v_ref, o_ref, do_ref, lse_ref, len_ref,
     dq_ref, dk_ref, dv_ref,
-    kvs, kvb, qb, dob, lsec, lset, lseb, dls, dlb, acc, dqt, dqs, dqr, pxs, pxr, rts, ret,
-    s_kv, s_kvn, r_kv, s_kvp, r_kvp, s_q, r_q, s_do, r_do,
+    kin, ov, dov, kvs, kvb, qb, dob, lset, lseb, dls, dlb, acc, dqt, dqs, dqr, pxs, pxr, rts, ret,
+    s_in, s_kv, s_kvn, r_kv, s_kvp, r_kvp, s_q, r_q, s_do, r_do,
     s_l, r_l, s_d, r_d, s_dq, r_dq, s_px, r_px, s_rt, s_rtp, r_rt, r_rtn,
 ):
     z = lax.axis_index("head")
@@ -71,9 +71,44 @@
             for e in range(4):
                 pl.semaphore_signal(barrier, inc=1, device_id=(zx(e), at(1, a, 0)), device_id_type=MESH)
 
+    loads = [
+        pltpu.make_async_copy(src, dst, s_in.at[n])
+        for n, (src, dst) in enumerate(
+            ((k_ref.at[0], kin.at[0]), (v_ref.at[0], kin.at[1]), (lse_ref.at[0], lset), (do_ref.at[0], dov), (o_ref.at[0], ov))
+        )
+    ]
+    for load in loads:
+        load.start()
+    acc[...] = jnp.zeros_like(acc)
+
+    place = lax.broadcasted_iota(jnp.int32, (8, 128), 1) + (pair * 1024 + zp * 128)
+
+    def block_of(j):
+        return 2 * ((xq + j // 2) % 2) + (core + j % 2) % 2
+
+    def seek(d, carry):
+        begin, found = carry
+        found = tuple(jnp.where(place + 256 * block_of(n) >= begin, begin, f) for n, f in enumerate(found))
+        return begin + len_ref[d], found
+
+    _, opens = lax.fori_loop(0, 64, seek, (jnp.int32(0), tuple(jnp.zeros((8, 128), jnp.int32) for _ in range(4))))
+
+    for load in loads[:2]:
+        load.wait()
     for n in range(4):
-        kvs[:, n * 256 : n * 256 + 128] = k_ref[0, :, n * 128 : (n + 1) * 128]
-        kvs[:, n * 256 + 128 : (n + 1) * 256] = v_ref[0, :, n * 128 : (n + 1) * 128]
+        kvs[:, n * 256 : n * 256 + 128] = kin[0, :, n * 128 : (n + 1) * 128]
+        kvs[:, n * 256 + 128 : (n + 1) * 256] = kin[1, :, n * 128 : (n + 1) * 128]
+
+    for load in loads[2:]:
+        load.wait()
+    lanes = lax.broadcasted_iota(jnp.int32, (64, 128), 1)
+    delta = jnp.zeros((64, 128), F32)
+    for n in range(32):
+        part = dov[:, n * 128 : (n + 1) * 128].astype(F32) * ov[:, n * 128 : (n + 1) * 128].astype(F32)
+        delta = jnp.where(lanes == n, jnp.sum(part, axis=1, keepdims=True), delta)
+    both = jnp.concatenate([delta, delta], axis=0).T
+    for n in range(4):
+        dls[n] = both[n * 8 : (n + 1) * 8]
 
     pl.semaphore_wait(barrier, 15 + 8 * ((pair + GROUPS - 1) // GROUPS) + 8 * ((2 * GROUPS - 2 - pair) // GROUPS))
 
@@ -95,7 +130,6 @@
     def _():
         send_kv(1)
 
-    rows_own = pl.ds(pl.multiple_of(own * 128 + zb * 64, 64), 64)
     for a in range(2):
         for b in range(2):
             for e in range(2):
@@ -103,64 +137,44 @@
                 cols = pl.ds(pl.multiple_of(lane, 512), 512)
                 for ref, buf, ss, rr in ((q_ref, qb, s_q, r_q), (do_ref, dob, s_do, r_do)):
                     src = ref.at[0, :, cols]
-                    dst = buf.at[rows_own]
+                    slot = 2 * a + b
+                    dst = buf.at[pl.ds(pl.multiple_of(slot * 128 + zb * 64, 64), 64)]
                     if a or b or e:
-                        remote(src, dst, ss, rr.at[own], (zx(e), at(0, a, b))).start()
+                        remote(src, dst, ss, rr.at[slot], (zx(e), at(0, a, b))).start()
                     else:
-                        pltpu.make_async_copy(src, dst, rr.at[own]).start()
-
-    lsec[...] = jnp.zeros_like(lsec)
-    lsec[:, 0:8] = lse_ref[0]
-    turned = lsec[...].T
-    for p in range(2):
-        lset[p] = turned[0:8, p * 128 : (p + 1) * 128]
+                        pltpu.make_async_copy(src, dst, rr.at[slot]).start()
+
     to_x = z // 2
     for e in (0, 2):
         half = zx(e) // 2
         for b in range(2):
             dev = (zx(e), 4 * pair + 2 * to_x + kx(b))
-            src, dst = lset.at[half], lseb.at[own]
+            slot = 2 * ((to_x + xq) % 2) + b
+            src, dst = lset.at[:, pl.ds(pl.multiple_of(half * 128, 128), 128)], lseb.at[slot]
             if e == 0 and b == 0:
                 @pl.when(to_x == xq)
                 def _():
-                    pltpu.make_async_copy(src, dst, r_l.at[own]).start()
+                    pltpu.make_async_copy(src, dst, r_l.at[slot]).start()
 
                 @pl.when(to_x != xq)
                 def _():
-                    remote(src, dst, s_l.at[0], r_l.at[own], dev).start()
+                    remote(src, dst, s_l.at[0], r_l.at[slot], dev).start()
             else:
-                remote(src, dst, s_l.at[e + b], r_l.at[own], dev).start()
-
-    lanes = lax.broadcasted_iota(jnp.int32, (64, 128), 1)
-    delta = jnp.zeros((64, 128), F32)
-    for n in range(32):
-        part = do_ref[0, :, n * 128 : (n + 1) * 128].astype(F32) * o_ref[0, :, n * 128 : (n + 1) * 128].astype(F32)
-        delta = jnp.where(lanes == n, jnp.sum(part, axis=1, keepdims=True), delta)
-    both = jnp.concatenate([delta, delta], axis=0).T
-    for n in range(4):
-        dls[n] = both[n * 8 : (n + 1) * 8]
+                remote(src, dst, s_l.at[e + b], r_l.at[slot], dev).start()
+
     for a in range(2):
         for b in range(2):
             for e in range(2):
                 src = dls.at[2 * xx(a) + zx(e) % 2]
-                dst = dlb.at[pl.ds(pl.multiple_of(own * 16 + zb * 8, 8), 8)]
+                slot = 2 * a + b
+                dst = dlb.at[pl.ds(pl.multiple_of(slot * 16 + zb * 8, 8), 8)]
                 if a or b or e:
-                    remote(src, dst, s_d, r_d.at[own], (zx(e), at(0, a, b))).start()
+                    remote(src, dst, s_d, r_d.at[slot], (zx(e), at(0, a, b))).start()
                 else:
-                    pltpu.make_async_copy(src, dst, r_d.at[own]).start()
-
-    place = lax.broadcasted_iota(jnp.int32, (8, 128), 1) + (pair * 1024 + zp * 128)
-
-    def seek(d, carry):
-        begin, found = carry
-        found = tuple(jnp.where(place + 256 * n >= begin, begin, f) for n, f in enumerate(found))
-        return begin + len_ref[d], found
-
-    _, opens = lax.fori_loop(0, 64, seek, (jnp.int32(0), tuple(jnp.zeros((8, 128), jnp.int32) for _ in range(4))))
+                    pltpu.make_async_copy(src, dst, r_d.at[slot]).start()
+
     for n in range(4):
         dqt[n] = jnp.zeros((128, 512), F32)
-    acc[...] = jnp.zeros_like(acc)
-
     @pl.when(first)
     def _():
         kvb[0:1024] = jnp.zeros((1024, 256), BF16)
@@ -191,35 +205,25 @@
         else:
             take()
 
-    for n in range(4):
-        await_bytes(lseb.at[n], r_l.at[n])
-        await_bytes(dlb.at[n * 16 : n * 16 + 16], r_d.at[n])
-        await_bytes(qb.at[n * 128 : n * 128 + 128], r_q.at[n])
-        await_bytes(dob.at[n * 128 : n * 128 + 128], r_do.at[n])
     steps = lax.broadcasted_iota(jnp.int32, (256, 128), 0)
     low = lax.broadcasted_iota(jnp.int32, (8, 128), 1) < 64
 
-    def piece(j):
-        bx = (xq + j // 2) % 2
-        bk = (core + j % 2) % 2
-        bi = 2 * bx + bk
-        mine = pl.ds(pl.multiple_of(bi * 128, 128), 128)
-        deltas = dlb.at[pl.ds(pl.multiple_of(bi * 16, 16), 16)]
-        lse_all = lseb[bi]
-        delta_all = jnp.where(low, deltas[0:8], deltas[8:16])
+    def work(j, begin, end):
+        bi = block_of(j)
+        lse_all = lseb[j]
+        delta_all = jnp.where(low, dlb[j * 16 : j * 16 + 8], dlb[j * 16 + 8 : j * 16 + 16])
         lse_mine = jnp.where(core == 0, lse_all[0:4], lse_all[4:8])
         delta_mine = jnp.where(core == 0, delta_all[0:4], delta_all[4:8])
         lse_row = jnp.concatenate([lse_mine[n : n + 1] for n in range(4)], axis=1)
         delta_row = jnp.concatenate([delta_mine[n : n + 1] for n in range(4)], axis=1)
-        where_open = jnp.where(bi == 0, opens[0], jnp.where(bi == 1, opens[1], jnp.where(bi == 2, opens[2], opens[3])))[0:1]
+        where_open = opens[j][0:1]
         where_here = (place + 256 * bi)[0:1]
-        qp = qb[mine]
-        dop = dob[mine]
+        qp = qb[j * 128 : (j + 1) * 128]
+        dop = dob[j * 128 : (j + 1) * 128]
         qm = jnp.concatenate([qp[:, n * 128 : (n + 1) * 128] for n in range(4)], axis=0)
         dom = jnp.concatenate([dop[:, n * 128 : (n + 1) * 128] for n in range(4)], axis=0)
 
-        def lag(l, _):
-            b = bi + l
+        def lag(b, _):
             rows = blk(b)
             key = kvb[rows, 0:128]
             value = kvb[rows, 128:256]
@@ -232,33 +236,36 @@
             shifted = (weights * (grads - delta_row) * SCALE).astype(BF16)
             acc[rows, 128:256] += jnp.dot(weights.astype(BF16), dom, preferred_element_type=F32)
             acc[rows, 0:128] += jnp.dot(shifted, qm, preferred_element_type=F32)
-            dqt[bi] += lax.dot_general(key, shifted, (((0,), (0,)), ((), ())), preferred_element_type=F32)
+            dqt[j] += lax.dot_general(key, shifted, (((0,), (0,)), ((), ())), preferred_element_type=F32)
             return 0
 
-        lax.fori_loop(0, 5, lag, 0)
-        done = dqt[bi]
+        lax.fori_loop(begin, end, lag, 0)
+
+    def arrived(j):
+        await_bytes(lseb.at[j], r_l.at[j])
+        await_bytes(dlb.at[j * 16 : (j + 1) * 16], r_d.at[j])
+        await_bytes(qb.at[j * 128 : (j + 1) * 128], r_q.at[j])
+        await_bytes(dob.at[j * 128 : (j + 1) * 128], r_do.at[j])
+
+    def hand_back(j):
         for n in range(4):
-            dqs[j * 128 : (j + 1) * 128, n * 128 : (n + 1) * 128] = done[:, n * 128 : (n + 1) * 128].T.astype(BF16)
-    slot = 2 * g + core
-    for j in range(4):
-        piece(j)
-    for j in range(4):
-        bx = (xq + j // 2) % 2
-        bk = (core + j % 2) % 2
-        bi = 2 * bx + bk
-        for e in range(2):
+            dqs[j * 128 : (j + 1) * 128, n * 128 : (n + 1) * 128] = dqt[j, :, n * 128 : (n + 1) * 128].T.astype(BF16)
+        slot = 2 * g + core
+        for e in (1, 0):
             src = dqs.at[pl.ds(pl.multiple_of(j * 128 + (zx(e) % 2) * 64, 64), 64)]
             dst = dqr.at[slot]
-            if e:
-                remote(src, dst, s_dq, r_dq, (zx(1), 4 * pair + bi)).start()
-            elif j:
-                remote(src, dst, s_dq, r_dq, (z, 4 * pair + bi)).start()
+            if e or j:
+                remote(src, dst, s_dq, r_dq, (zx(e), 4 * pair + block_of(j))).start()
             else:
                 pltpu.make_async_copy(src, dst, r_dq).start()
 
-    for i in range(4):
+    def to_partner(i):
         pxs[i] = acc[blk(2 * i + 1 - core)].astype(BF16)
         remote(pxs.at[i], pxr.at[i], s_px, r_px.at[i], partner).start()
+
+    def from_partner(i):
+        await_bytes(pxr.at[i], r_px.at[i])
+        rts[i] = (acc[blk(2 * i + core)] + pxr[i].astype(F32)).astype(BF16)
 
     def send_back(off):
         for a in range(2):
@@ -271,17 +278,30 @@
                 else:
                     remote(src, dst, s_rtp if off else s_rt, r_rtn if off else r_rt, (zx(e), at(-off, a, 0))).start()
 
+    for j in range(2):
+        arrived(j)
+        work(j, block_of(j), block_of(j) + 5)
+        hand_back(j)
+    for j in range(2, 4):
+        arrived(j)
+        work(j, block_of(j), 4)
     for i in range(2):
-        await_bytes(pxr.at[i], r_px.at[i])
-        rts[i] = (acc[blk(2 * i + core)] + pxr[i].astype(F32)).astype(BF16)
+        to_partner(i)
+    work(2, 4, block_of(2) + 5)
+    hand_back(2)
+    for i in range(2):
+        from_partner(i)
 
     @pl.when(jnp.logical_not(first))
     def _():
         send_back(1)
 
+    work(3, 4, block_of(3) + 5)
     for i in range(2, 4):
-        await_bytes(pxr.at[i], r_px.at[i])
-        rts[i] = (acc[blk(2 * i + core)] + pxr[i].astype(F32)).astype(BF16)
+        to_partner(i)
+    hand_back(3)
+    for i in range(2, 4):
+        from_partner(i)
     send_back(0)
 
     await_bytes(ret.at[0:8], r_rt)
@@ -314,11 +334,11 @@
     await_bytes(ret.at[0:7], s_rt)
     await_bytes(dlb.at[0 : 7 * 8], s_d)
     for n in range(1, 4):
-        await_bytes(lset.at[0], s_l.at[n])
+        await_bytes(lseb.at[0], s_l.at[n])
 
     @pl.when(to_x != xq)
     def _():
-        await_bytes(lset.at[0], s_l.at[0])
+        await_bytes(lseb.at[0], s_l.at[0])
 
     @pl.when(jnp.logical_not(last))
     def _():
@@ -336,6 +356,7 @@
 
 def local(queries, keys, values, outputs, gradient, sums, lengths):
     vmem = pl.BlockSpec(memory_space=pltpu.VMEM)
+    hbm = pl.BlockSpec(memory_space=pltpu.HBM)
     dma = pltpu.SemaphoreType.DMA
     return pl.pallas_call(
         kernel,
@@ -344,15 +365,17 @@
             jax.ShapeDtypeStruct((1, 64, 512), BF16),
             jax.ShapeDtypeStruct((1, 64, 512), BF16),
         ),
-        in_specs=[vmem] * 6 + [pl.BlockSpec(memory_space=pltpu.SMEM)],
+        in_specs=[hbm] * 6 + [pl.BlockSpec(memory_space=pltpu.SMEM)],
         out_specs=(vmem, vmem, vmem),
         scratch_shapes=[
+            pltpu.VMEM((2, 64, 512), BF16),
+            pltpu.VMEM((64, 4096), BF16),
+            pltpu.VMEM((64, 4096), BF16),
             pltpu.VMEM((64, 1024), BF16),
             pltpu.VMEM((2048, 256), BF16),
             pltpu.VMEM((512, 512), BF16),
             pltpu.VMEM((512, 512), BF16),
-            pltpu.VMEM((256, 128), F32),
-            pltpu.VMEM((2, 8, 128), F32),
+            pltpu.VMEM((8, 256), F32),
             pltpu.VMEM((4, 8, 128), F32),
             pltpu.VMEM((4, 8, 128), F32),
             pltpu.VMEM((64, 128), F32),
@@ -364,14 +387,14 @@
             pltpu.VMEM((4, 256, 256), BF16),
             pltpu.VMEM((4, 256, 256), BF16),
             pltpu.VMEM((16, 64, 256), BF16),
-            dma, dma, dma((8,)), dma, dma((8,)), dma, dma((4,)), dma, dma((4,)),
+            dma((5,)), dma, dma, dma((8,)), dma, dma((8,)), dma, dma((4,)), dma, dma((4,)),
             dma((4,)), dma((4,)), dma, dma((4,)), dma, dma, dma, dma((4,)), dma, dma, dma, dma,
         ],
         compiler_params=pltpu.CompilerParams(
-            collective_id=0, has_side_effects=True, vmem_limit_bytes=48 * 2**20
+            collective_id=0, has_side_effects=True, vmem_limit_bytes=63 * 2**20
         ),
         name="attention_backward",
-    )(queries, keys, values, outputs, gradient, sums, lengths)
+    )(queries, keys, values, outputs, gradient, jnp.transpose(sums, (0, 2, 1)), lengths)
 
 
 def solution(mesh):

time: 69.7 us -> 63.8 us (0.915)
  the two profiles are of different devices: /device:TPU:60 before, /device:TPU:28 now
where the time goes in v1:
time: 63.8 us; the launch traced here: 63.6 us
  Pallas kernels  59.6 us (93%)
  local copies, waits for them, and re-layouts  3.4 us (5%)
  between operations  0.65 us (1%)
    pallas_call x1, Pallas kernels, local(): pl.pallas_call(kernel, out_shape=(jax.ShapeDtypeStruct((1, 64, 4096), BF1...  59.6 us
    unnamed x7, local copies, waits for them, and re-layouts  3.4 us

profile of v1, /device:TPU:28, one launch (start us, length us, event | category | flops | bytes accessed | tf_op | source)
XLA Modules:
  0.0 63.6 jit_solution(3458816214636592211)
XLA Ops:
  0.6 59.6 %attention_backward.1 = (bf16[1,64,4096]{2,1,0:T(8,128)(2,1)}, bf16[1,64,512]{2,1,0:T(8,128)(2,1)}, bf16[1,64,512]{2,1,0:T(8,128)(2,1)}) custom-call(bf16[1,64,4096]{2,1,0:T(8,128)(2,1)} %q_ref.1, bf16[1,64,512]{2,1,0:T(8,128)(2,1)} %k_ref.1, bf16[1,64,512]{2,1,0:T(8,128)(2,1)} %v_ref.1, bf16[1,64,4096]{2,1,0:T(8,128)(2,1)} %o_ref.1, ...), custom_call_target="tpu_custom_call" | custom-call | tf_op jit(solution)/shard_map/attention_backward/pallas_call | solution.py:361
  60.2 0.0 copy-start.1
  60.2 1.9 %copy.13 = bf16[1,64,4096]{2,1,0:T(8,128)(2,1)} copy(bf16[1,64,4096]{2,1,0:T(8,128)(2,1)} %get-tuple-element.6) | data formatting | bytes 1048576
  62.1 0.0 copy-done.1
  62.1 0.0 copy-start
  62.1 0.6 copy.14
  62.8 0.2 copy-done
  63.0 0.6 copy.15
Async XLA Ops:
  60.2 1.9 %copy-start.1 = (bf16[1,64,512]{2,1,0:T(8,128)(2,1)S(1)}, bf16[1,64,512]{2,1,0:T(8,128)(2,1)}, u32[]{:S(2)}) copy-start(bf16[1,64,512]{2,1,0:T(8,128)(2,1)} %get-tuple-element.7) | copy-start | bytes 196612
  62.1 0.9 %copy-start = (bf16[1,64,512]{2,1,0:T(8,128)(2,1)S(1)}, bf16[1,64,512]{2,1,0:T(8,128)(2,1)}, u32[]{:S(2)}) copy-start(bf16[1,64,512]{2,1,0:T(8,128)(2,1)} %get-tuple-element.8) | copy-start | bytes 196612

commit v2 on v1

--- a/solution.py
+++ b/solution.py
@@ -15,9 +15,9 @@
 def kernel(
     q_ref, k_ref, v_ref, o_ref, do_ref, lse_ref, len_ref,
     dq_ref, dk_ref, dv_ref,
-    kin, ov, dov, kvs, kvb, qb, dob, lset, lseb, dls, dlb, acc, dqt, dqs, dqr, pxs, pxr, rts, ret,
-    s_in, s_kv, s_kvn, r_kv, s_kvp, r_kvp, s_q, r_q, s_do, r_do,
-    s_l, r_l, s_d, r_d, s_dq, r_dq, s_px, r_px, s_rt, s_rtp, r_rt, r_rtn,
+    kin, ov, dov, kvs, kva, kvb, qb, dob, lset, lseb, dls, dlb, acc, dqt, dqs, dqr, pxs, pxr, rts, twin, via, ret,
+    s_in, s_kv, s_kvn, r_kva, r_kvb, s_pa, r_pa, s_pb, r_pb, s_q, r_q, s_do, r_do,
+    s_l, r_l, s_d, r_d, s_dq, r_dq, s_px, r_px, s_rt, s_rtp, r_rt, r_rtn, s_twin, r_twin, s_via, r_via,
 ):
     z = lax.axis_index("head")
     c = lax.axis_index("ctx")
@@ -30,6 +30,9 @@
     g = 2 * xq + zb
     first = pair == 0
     last = pair == GROUPS - 1
+    before = pair == GROUPS // 2 - 1
+    after = pair == GROUPS // 2
+    bridge = before | after | first | last
 
     def zx(e):
         return (z, z + 1 - 2 * zb, (z + 2) % 4, 3 - z)[e]
@@ -70,6 +73,18 @@
         for a in range(2):
             for e in range(4):
                 pl.semaphore_signal(barrier, inc=1, device_id=(zx(e), at(1, a, 0)), device_id_type=MESH)
+
+    def greet(e, to):
+        pl.semaphore_signal(barrier, inc=1, device_id=(zx(e), to), device_id_type=MESH)
+
+    across = own + 4 * jnp.where(before, GROUPS - 1, jnp.where(last, GROUPS // 2 - 1, jnp.where(after, 0, GROUPS // 2)))
+    aside = 2 * (1 - xq) + core + 4 * jnp.where(before, 0, jnp.where(first, GROUPS // 2 - 1, jnp.where(after, GROUPS - 1, GROUPS // 2)))
+
+    @pl.when(bridge)
+    def _():
+        for e in range(4):
+            greet(e, across)
+        greet(0, aside)
 
     loads = [
         pltpu.make_async_copy(src, dst, s_in.at[n])
@@ -110,26 +125,66 @@
     for n in range(4):
         dls[n] = both[n * 8 : (n + 1) * 8]
 
-    pl.semaphore_wait(barrier, 15 + 8 * ((pair + GROUPS - 1) // GROUPS) + 8 * ((2 * GROUPS - 2 - pair) // GROUPS))
+    pl.semaphore_wait(barrier, 15 + 8 * ((pair + GROUPS - 1) // GROUPS) + 8 * ((2 * GROUPS - 2 - pair) // GROUPS) + jnp.where(bridge, 5, 0))
+
+    rows_own = pl.ds(pl.multiple_of(own * 256 + z * 64, 64), 64)
 
     def send_kv(off):
-        slot = 4 * (1 - off) + own
         for a in range(2):
             for e in range(4):
                 there = 2 * xx(a) + zx(e) % 2
                 src = kvs.at[:, pl.ds(pl.multiple_of(there * 256, 256), 256)]
-                dst = kvb.at[pl.ds(pl.multiple_of(slot * 256 + z * 64, 64), 64)]
-                if off == 0 and a == 0 and e == 0:
-                    pltpu.make_async_copy(src, dst, r_kv.at[slot]).start()
+                if off:
+                    remote(src, kva.at[rows_own], s_kvn, r_kva.at[own], (zx(e), at(1, a, 0))).start()
+                elif a or e:
+                    remote(src, kvb.at[rows_own], s_kv, r_kvb.at[own], (zx(e), at(0, a, 0))).start()
                 else:
-                    remote(src, dst, s_kvn if off else s_kv, r_kv.at[slot], (zx(e), at(off, a, 0))).start()
+                    pltpu.make_async_copy(src, kvb.at[rows_own], r_kvb.at[own]).start()
+
+    @pl.when(before)
+    def _():
+        for e in range(4):
+            src = kvs.at[:, pl.ds(pl.multiple_of((2 * xq + zx(e) % 2) * 256, 256), 256)]
+            remote(src, kva.at[rows_own], s_kvn, r_kva.at[own], (zx(e), at(1, 0, 0))).start()
+        src = kvs.at[:, pl.ds(pl.multiple_of((1 - xq) * 512, 512), 512)]
+        remote(src, twin, s_twin, r_twin, (z, aside)).start()
 
     send_kv(0)
 
-    @pl.when(jnp.logical_not(last))
+    @pl.when(jnp.logical_not(last | before))
     def _():
         send_kv(1)
 
+    to_x = z // 2
+    for e in (0, 2):
+        half = zx(e) // 2
+        for b in range(2):
+            dev = (zx(e), 4 * pair + 2 * to_x + kx(b))
+            slot = 2 * ((to_x + xq) % 2) + b
+            src, dst = lset.at[:, pl.ds(pl.multiple_of(half * 128, 128), 128)], lseb.at[slot]
+            if e == 0 and b == 0:
+                @pl.when(to_x == xq)
+                def _():
+                    pltpu.make_async_copy(src, dst, r_l.at[slot]).start()
+
+                @pl.when(to_x != xq)
+                def _():
+                    remote(src, dst, s_l.at[0], r_l.at[slot], dev).start()
+            else:
+                remote(src, dst, s_l.at[e + b], r_l.at[slot], dev).start()
+
+    for a in range(2):
+        for b in range(2):
+            for e in range(2):
+                src = dls.at[2 * xx(a) + zx(e) % 2]
+                slot = 2 * a + b
+                dst = dlb.at[pl.ds(pl.multiple_of(slot * 16 + zb * 8, 8), 8)]
+                if a or b or e:
+                    remote(src, dst, s_d, r_d.at[slot], (zx(e), at(0, a, b))).start()
+                else:
+                    pltpu.make_async_copy(src, dst, r_d.at[slot]).start()
+
+    await_bytes(kvb.at[0 : 7 * 64], s_kv)
     for a in range(2):
         for b in range(2):
             for e in range(2):
@@ -144,72 +199,52 @@
                     else:
                         pltpu.make_async_copy(src, dst, rr.at[slot]).start()
 
-    to_x = z // 2
-    for e in (0, 2):
-        half = zx(e) // 2
-        for b in range(2):
-            dev = (zx(e), 4 * pair + 2 * to_x + kx(b))
-            slot = 2 * ((to_x + xq) % 2) + b
-            src, dst = lset.at[:, pl.ds(pl.multiple_of(half * 128, 128), 128)], lseb.at[slot]
-            if e == 0 and b == 0:
-                @pl.when(to_x == xq)
-                def _():
-                    pltpu.make_async_copy(src, dst, r_l.at[slot]).start()
-
-                @pl.when(to_x != xq)
-                def _():
-                    remote(src, dst, s_l.at[0], r_l.at[slot], dev).start()
-            else:
-                remote(src, dst, s_l.at[e + b], r_l.at[slot], dev).start()
-
-    for a in range(2):
-        for b in range(2):
-            for e in range(2):
-                src = dls.at[2 * xx(a) + zx(e) % 2]
-                slot = 2 * a + b
-                dst = dlb.at[pl.ds(pl.multiple_of(slot * 16 + zb * 8, 8), 8)]
-                if a or b or e:
-                    remote(src, dst, s_d, r_d.at[slot], (zx(e), at(0, a, b))).start()
-                else:
-                    pltpu.make_async_copy(src, dst, r_d.at[slot]).start()
-
     for n in range(4):
         dqt[n] = jnp.zeros((128, 512), F32)
-    @pl.when(first)
-    def _():
-        kvb[0:1024] = jnp.zeros((1024, 256), BF16)
-
     def blk(b):
         return pl.ds(pl.multiple_of(b * 256, 256), 256)
 
     partner = (z, at(0, 0, 1))
-    for i in range(4):
+
+    def hand_on(buf, sent, got, i):
         b = 2 * i + core
-
-        def hand_on():
-            await_bytes(kvb.at[blk(b)], r_kv.at[b])
-            remote(kvb.at[blk(b)], kvb.at[blk(b)], s_kvp, r_kvp.at[b], partner).start()
-
-        if i < 2:
-            pl.when(jnp.logical_not(first))(hand_on)
-        else:
-            hand_on()
-    for i in range(4):
-        b = 2 * i + 1 - core
-
-        def take():
-            await_bytes(kvb.at[blk(b)], r_kvp.at[b])
-
-        if i < 2:
-            pl.when(jnp.logical_not(first))(take)
-        else:
-            take()
+        remote(buf.at[blk(b)], buf.at[blk(b)], sent, got.at[b], partner).start()
+
+    def own_blocks():
+        for i in range(2):
+            await_bytes(kvb.at[blk(2 * i + core)], r_kvb.at[2 * i + core])
+            hand_on(kvb, s_pb, r_pb, i)
+        for i in range(2):
+            await_bytes(kvb.at[blk(2 * i + 1 - core)], r_pb.at[2 * i + 1 - core])
+
+    def earlier_blocks():
+        @pl.when(first)
+        def _():
+            kva[...] = jnp.zeros_like(kva)
+
+        @pl.when(first)
+        def _():
+            await_bytes(twin, r_twin)
+            theirs = 2 * (1 - xq) + core
+            dst = kva.at[pl.ds(pl.multiple_of(theirs * 256 + z * 64, 64), 64)]
+            for e in range(4):
+                src = twin.at[:, pl.ds(pl.multiple_of(zx(e) % 2 * 256, 256), 256)]
+                remote(src, dst, s_via, r_kva.at[theirs], (zx(e), across)).start()
+
+        @pl.when(jnp.logical_not(first))
+        def _():
+            for i in range(2):
+                await_bytes(kva.at[blk(2 * i + core)], r_kva.at[2 * i + core])
+                hand_on(kva, s_pa, r_pa, i)
+            for i in range(2):
+                await_bytes(kva.at[blk(2 * i + 1 - core)], r_pa.at[2 * i + 1 - core])
 
     steps = lax.broadcasted_iota(jnp.int32, (256, 128), 0)
     low = lax.broadcasted_iota(jnp.int32, (8, 128), 1) < 64
 
-    def work(j, begin, end):
+    def work(j, buf):
         bi = block_of(j)
+        ahead = 4 if buf is kvb else 0
         lse_all = lseb[j]
         delta_all = jnp.where(low, dlb[j * 16 : j * 16 + 8], dlb[j * 16 + 8 : j * 16 + 16])
         lse_mine = jnp.where(core == 0, lse_all[0:4], lse_all[4:8])
@@ -224,10 +259,10 @@
         dom = jnp.concatenate([dop[:, n * 128 : (n + 1) * 128] for n in range(4)], axis=0)
 
         def lag(b, _):
-            rows = blk(b)
-            key = kvb[rows, 0:128]
-            value = kvb[rows, 128:256]
-            base = (4 * pair - 4 + b) * 256
+            rows = blk(b + ahead)
+            key = buf[blk(b), 0:128]
+            value = buf[blk(b), 128:256]
+            base = (4 * pair - 4 + ahead + b) * 256
             allowed = (steps >= where_open - base) & (steps <= where_here - base)
             allowed = jnp.concatenate([allowed] * 4, axis=1)
             scores = lax.dot_general(key, qm, (((1,), (1,)), ((), ())), preferred_element_type=F32)
@@ -239,7 +274,7 @@
             dqt[j] += lax.dot_general(key, shifted, (((0,), (0,)), ((), ())), preferred_element_type=F32)
             return 0
 
-        lax.fori_loop(begin, end, lag, 0)
+        lax.fori_loop(0 if ahead else bi, bi + 1 if ahead else 4, lag, 0)
 
     def arrived(j):
         await_bytes(lseb.at[j], r_l.at[j])
@@ -272,31 +307,43 @@
             i = (2 * (1 - off)) + xx(a)
             for e in range(4):
                 src = rts.at[i, pl.ds(pl.multiple_of(zx(e) * 64, 64), 64)]
-                dst = ret.at[off * 8 + z * 2 + xq]
+                dst = ret.at[off * 8 + xq * 4 + z]
                 if off == 0 and a == 0 and e == 0:
                     pltpu.make_async_copy(src, dst, r_rt).start()
                 else:
-                    remote(src, dst, s_rtp if off else s_rt, r_rtn if off else r_rt, (zx(e), at(-off, a, 0))).start()
-
+                    remote(src, dst, s_rtp if off else s_rt, r_rtn.at[xq] if off else r_rt, (zx(e), at(-off, a, 0))).start()
+
+    own_blocks()
     for j in range(2):
         arrived(j)
-        work(j, block_of(j), block_of(j) + 5)
+        work(j, kvb)
+    earlier_blocks()
+    for j in range(2):
+        work(j, kva)
         hand_back(j)
     for j in range(2, 4):
         arrived(j)
-        work(j, block_of(j), 4)
+        work(j, kva)
     for i in range(2):
         to_partner(i)
-    work(2, 4, block_of(2) + 5)
-    hand_back(2)
+    work(2, kvb)
     for i in range(2):
         from_partner(i)
 
-    @pl.when(jnp.logical_not(first))
+    @pl.when(jnp.logical_not(first | after))
     def _():
         send_back(1)
 
-    work(3, 4, block_of(3) + 5)
+    @pl.when(after)
+    def _():
+        for e in range(4):
+            part = pl.ds(pl.multiple_of(zx(e) * 64, 64), 64)
+            remote(rts.at[xq, part], ret.at[8 + xq * 4 + z], s_rtp, r_rtn.at[xq], (zx(e), at(-1, 0, 0))).start()
+        remote(rts.at[1 - xq], via, s_twin, r_via, (z, aside)).start()
+
+    hand_back(2)
+    work(3, kvb)
+
     for i in range(2, 4):
         to_partner(i)
     hand_back(3)
@@ -304,6 +351,13 @@
         from_partner(i)
     send_back(0)
 
+    @pl.when(last)
+    def _():
+        await_bytes(via, r_via)
+        for e in range(4):
+            src = via.at[pl.ds(pl.multiple_of(zx(e) * 64, 64), 64)]
+            remote(src, ret.at[8 + (1 - xq) * 4 + z], s_via, r_rtn.at[1 - xq], (zx(e), across)).start()
+
     await_bytes(ret.at[0:8], r_rt)
 
     @pl.when(last)
@@ -312,13 +366,14 @@
 
     @pl.when(jnp.logical_not(last))
     def _():
-        await_bytes(ret.at[8:16], r_rtn)
+        await_bytes(ret.at[8:12], r_rtn.at[0])
+        await_bytes(ret.at[12:16], r_rtn.at[1])
 
     for n in range(4):
         total = jnp.zeros((64, 256), F32)
         for off in range(2):
             for p in range(2):
-                total = total + ret[off * 8 + (2 * p + n % 2) * 2 + n // 2].astype(F32)
+                total = total + ret[off * 8 + (n // 2) * 4 + 2 * p + n % 2].astype(F32)
         dk_ref[0, :, n * 128 : (n + 1) * 128] = total[:, 0:128].astype(BF16)
         dv_ref[0, :, n * 128 : (n + 1) * 128] = total[:, 128:256].astype(BF16)
 
@@ -326,7 +381,6 @@
     for n in range(8):
         dq_ref[0, :, n * 512 : (n + 1) * 512] = dqr[n]
 
-    await_bytes(kvb.at[0 : 7 * 64], s_kv)
     await_bytes(qb.at[0 : 7 * 64], s_q)
     await_bytes(dob.at[0 : 7 * 64], s_do)
     await_bytes(dqs.at[0 : 7 * 64], s_dq)
@@ -340,18 +394,33 @@
     def _():
         await_bytes(lseb.at[0], s_l.at[0])
 
-    @pl.when(jnp.logical_not(last))
+    @pl.when(before)
+    def _():
+        await_bytes(kvb.at[0:256], s_kvn)
+        await_bytes(twin, s_twin)
+
+    @pl.when(jnp.logical_not(last | before))
     def _():
         await_bytes(kvb.at[0:512], s_kvn)
 
-    @pl.when(first)
-    def _():
-        await_bytes(kvb.at[0:512], s_kvp)
+    await_bytes(kvb.at[0:512], s_pb)
 
     @pl.when(jnp.logical_not(first))
     def _():
-        await_bytes(kvb.at[0:1024], s_kvp)
+        await_bytes(kvb.at[0:512], s_pa)
+
+    @pl.when(after)
+    def _():
+        await_bytes(ret.at[0:4], s_rtp)
+        await_bytes(via, s_twin)
+
+    @pl.when(jnp.logical_not(first | after))
+    def _():
         await_bytes(ret.at[0:8], s_rtp)
+
+    @pl.when(first | last)
+    def _():
+        await_bytes(via, s_via)
 
 
 def local(queries, keys, values, outputs, gradient, sums, lengths):
@@ -372,7 +441,8 @@
             pltpu.VMEM((64, 4096), BF16),
             pltpu.VMEM((64, 4096), BF16),
             pltpu.VMEM((64, 1024), BF16),
-            pltpu.VMEM((2048, 256), BF16),
+            pltpu.VMEM((1024, 256), BF16),
+            pltpu.VMEM((1024, 256), BF16),
             pltpu.VMEM((512, 512), BF16),
             pltpu.VMEM((512, 512), BF16),
             pltpu.VMEM((8, 256), F32),
@@ -386,9 +456,12 @@
             pltpu.VMEM((4, 256, 256), BF16),
             pltpu.VMEM((4, 256, 256), BF16),
             pltpu.VMEM((4, 256, 256), BF16),
+            pltpu.VMEM((64, 512), BF16),
+            pltpu.VMEM((256, 256), BF16),
             pltpu.VMEM((16, 64, 256), BF16),
-            dma((5,)), dma, dma, dma((8,)), dma, dma((8,)), dma, dma((4,)), dma, dma((4,)),
-            dma((4,)), dma((4,)), dma, dma((4,)), dma, dma, dma, dma((4,)), dma, dma, dma, dma,
+            dma((5,)), dma, dma, dma((4,)), dma((4,)), dma, dma((4,)), dma, dma((4,)), dma, dma((4,)), dma, dma((4,)),
+            dma((4,)), dma((4,)), dma, dma((4,)), dma, dma, dma, dma((4,)), dma, dma, dma, dma((2,)),
+            dma, dma, dma, dma,
         ],
         compiler_params=pltpu.CompilerParams(
             collective_id=0, has_side_effects=True, vmem_limit_bytes=63 * 2**20

time: 63.8 us -> 61.6 us (0.966)
  the two profiles are of different devices: /device:TPU:28 before, /device:TPU:30 now
where the time goes in v2:
time: 61.6 us; the launch traced here: 61.5 us
  Pallas kernels  57.4 us (93%)
  local copies, waits for them, and re-layouts  3.4 us (6%)
  between operations  0.65 us (1%)
    pallas_call x1, Pallas kernels, local(): pl.pallas_call(kernel, out_shape=(jax.ShapeDtypeStruct((1, 64, 4096), BF1...  57.4 us
    unnamed x7, local copies, waits for them, and re-layouts  3.4 us

profile of v2, /device:TPU:30, one launch (start us, length us, event | category | flops | bytes accessed | tf_op | source)
XLA Modules:
  0.0 61.5 jit_solution(17021099603243523907)
XLA Ops:
  0.6 57.4 %attention_backward.1 = (bf16[1,64,4096]{2,1,0:T(8,128)(2,1)}, bf16[1,64,512]{2,1,0:T(8,128)(2,1)}, bf16[1,64,512]{2,1,0:T(8,128)(2,1)}) custom-call(bf16[1,64,4096]{2,1,0:T(8,128)(2,1)} %q_ref.1, bf16[1,64,512]{2,1,0:T(8,128)(2,1)} %k_ref.1, bf16[1,64,512]{2,1,0:T(8,128)(2,1)} %v_ref.1, bf16[1,64,4096]{2,1,0:T(8,128)(2,1)} %o_ref.1, ...), custom_call_target="tpu_custom_call" | custom-call | tf_op jit(solution)/shard_map/attention_backward/pallas_call | solution.py:430
  58.1 0.0 copy-start.1
  58.1 1.9 %copy.13 = bf16[1,64,4096]{2,1,0:T(8,128)(2,1)} copy(bf16[1,64,4096]{2,1,0:T(8,128)(2,1)} %get-tuple-element.6) | data formatting | bytes 1048576
  60.0 0.0 copy-done.1
  60.0 0.0 copy-start
  60.0 0.6 %copy.14 = bf16[1,64,512]{2,1,0:T(8,128)(2,1)} copy(bf16[1,64,512]{2,1,0:T(8,128)(2,1)S(1)} %copy-done.1) | data formatting | bytes 131072
  60.6 0.2 copy-done
  60.8 0.6 %copy.15 = bf16[1,64,512]{2,1,0:T(8,128)(2,1)} copy(bf16[1,64,512]{2,1,0:T(8,128)(2,1)S(1)} %copy-done) | data formatting | bytes 131072
Async XLA Ops:
  58.1 1.9 %copy-start.1 = (bf16[1,64,512]{2,1,0:T(8,128)(2,1)S(1)}, bf16[1,64,512]{2,1,0:T(8,128)(2,1)}, u32[]{:S(2)}) copy-start(bf16[1,64,512]{2,1,0:T(8,128)(2,1)} %get-tuple-element.7) | copy-start | bytes 196612
  60.0 0.9 %copy-start = (bf16[1,64,512]{2,1,0:T(8,128)(2,1)S(1)}, bf16[1,64,512]{2,1,0:T(8,128)(2,1)}, u32[]{:S(2)}) copy-start(bf16[1,64,512]{2,1,0:T(8,128)(2,1)} %get-tuple-element.8) | copy-start | bytes 196612

commit v3 on v2

--- a/solution.py
+++ b/solution.py
@@ -129,17 +129,15 @@
 
     rows_own = pl.ds(pl.multiple_of(own * 256 + z * 64, 64), 64)
 
-    def send_kv(off):
-        for a in range(2):
-            for e in range(4):
-                there = 2 * xx(a) + zx(e) % 2
-                src = kvs.at[:, pl.ds(pl.multiple_of(there * 256, 256), 256)]
-                if off:
-                    remote(src, kva.at[rows_own], s_kvn, r_kva.at[own], (zx(e), at(1, a, 0))).start()
-                elif a or e:
-                    remote(src, kvb.at[rows_own], s_kv, r_kvb.at[own], (zx(e), at(0, a, 0))).start()
-                else:
-                    pltpu.make_async_copy(src, kvb.at[rows_own], r_kvb.at[own]).start()
+    def send_kv(off, a, e):
+        there = 2 * xx(a) + zx(e) % 2
+        src = kvs.at[:, pl.ds(pl.multiple_of(there * 256, 256), 256)]
+        if off:
+            remote(src, kva.at[rows_own], s_kvn, r_kva.at[own], (zx(e), at(1, a, 0))).start()
+        elif a or e:
+            remote(src, kvb.at[rows_own], s_kv, r_kvb.at[own], (zx(e), at(0, a, 0))).start()
+        else:
+            pltpu.make_async_copy(src, kvb.at[rows_own], r_kvb.at[own]).start()
 
     @pl.when(before)
     def _():
@@ -149,11 +147,13 @@
         src = kvs.at[:, pl.ds(pl.multiple_of((1 - xq) * 512, 512), 512)]
         remote(src, twin, s_twin, r_twin, (z, aside)).start()
 
-    send_kv(0)
+    for a, e in ((0, 0), (0, 2), (1, 0), (0, 3), (1, 2), (0, 1), (1, 3), (1, 1)):
+        send_kv(0, a, e)
 
     @pl.when(jnp.logical_not(last | before))
     def _():
-        send_kv(1)
+        for a, e in ((0, 2), (1, 2), (0, 3), (1, 3), (0, 0), (0, 1), (1, 0), (1, 1)):
+            send_kv(1, a, e)
 
     to_x = z // 2
     for e in (0, 2):
@@ -184,20 +184,32 @@
                 else:
                     pltpu.make_async_copy(src, dst, r_d.at[slot]).start()
 
+    def send_queries(*which):
+        for a, b, e in which:
+            lane = (2 * xx(a) + zx(e) % 2) * 1024 + kx(b) * 512
+            cols = pl.ds(pl.multiple_of(lane, 512), 512)
+            for ref, buf, ss, rr in ((q_ref, qb, s_q, r_q), (do_ref, dob, s_do, r_do)):
+                src = ref.at[0, :, cols]
+                slot = 2 * a + b
+                dst = buf.at[pl.ds(pl.multiple_of(slot * 128 + zb * 64, 64), 64)]
+                if a or b or e:
+                    remote(src, dst, ss, rr.at[slot], (zx(e), at(0, a, b))).start()
+                else:
+                    pltpu.make_async_copy(src, dst, rr.at[slot]).start()
+
+    send_queries((0, 0, 0), (0, 1, 0))
+
+    @pl.when(first)
+    def _():
+        await_bytes(twin, r_twin)
+        theirs = 2 * (1 - xq) + core
+        dst = kva.at[pl.ds(pl.multiple_of(theirs * 256 + z * 64, 64), 64)]
+        for e in range(4):
+            src = twin.at[:, pl.ds(pl.multiple_of(zx(e) % 2 * 256, 256), 256)]
+            remote(src, dst, s_via, r_kva.at[theirs], (zx(e), across)).start()
+
+    send_queries((0, 0, 1), (1, 0, 0), (0, 1, 1), (1, 1, 0), (1, 0, 1), (1, 1, 1))
     await_bytes(kvb.at[0 : 7 * 64], s_kv)
-    for a in range(2):
-        for b in range(2):
-            for e in range(2):
-                lane = (2 * xx(a) + zx(e) % 2) * 1024 + kx(b) * 512
-                cols = pl.ds(pl.multiple_of(lane, 512), 512)
-                for ref, buf, ss, rr in ((q_ref, qb, s_q, r_q), (do_ref, dob, s_do, r_do)):
-                    src = ref.at[0, :, cols]
-                    slot = 2 * a + b
-                    dst = buf.at[pl.ds(pl.multiple_of(slot * 128 + zb * 64, 64), 64)]
-                    if a or b or e:
-                        remote(src, dst, ss, rr.at[slot], (zx(e), at(0, a, b))).start()
-                    else:
-                        pltpu.make_async_copy(src, dst, rr.at[slot]).start()
 
     for n in range(4):
         dqt[n] = jnp.zeros((128, 512), F32)
@@ -221,15 +233,6 @@
         @pl.when(first)
         def _():
             kva[...] = jnp.zeros_like(kva)
-
-        @pl.when(first)
-        def _():
-            await_bytes(twin, r_twin)
-            theirs = 2 * (1 - xq) + core
-            dst = kva.at[pl.ds(pl.multiple_of(theirs * 256 + z * 64, 64), 64)]
-            for e in range(4):
-                src = twin.at[:, pl.ds(pl.multiple_of(zx(e) % 2 * 256, 256), 256)]
-                remote(src, dst, s_via, r_kva.at[theirs], (zx(e), across)).start()
 
         @pl.when(jnp.logical_not(first))
         def _():
@@ -242,7 +245,7 @@
     steps = lax.broadcasted_iota(jnp.int32, (256, 128), 0)
     low = lax.broadcasted_iota(jnp.int32, (8, 128), 1) < 64
 
-    def work(j, buf):
+    def work(j, buf, count=None):
         bi = block_of(j)
         ahead = 4 if buf is kvb else 0
         lse_all = lseb[j]
@@ -274,7 +277,7 @@
             dqt[j] += lax.dot_general(key, shifted, (((0,), (0,)), ((), ())), preferred_element_type=F32)
             return 0
 
-        lax.fori_loop(0 if ahead else bi, bi + 1 if ahead else 4, lag, 0)
+        lax.fori_loop(0 if ahead else bi, (bi + 1 if count is None else count) if ahead else 4, lag, 0)
 
     def arrived(j):
         await_bytes(lseb.at[j], r_l.at[j])
@@ -326,7 +329,8 @@
         work(j, kva)
     for i in range(2):
         to_partner(i)
-    work(2, kvb)
+    pieces_left = block_of(2) + 1
+    work(2, kvb, jnp.where(after, 0, pieces_left))
     for i in range(2):
         from_partner(i)
 
@@ -340,6 +344,10 @@
             part = pl.ds(pl.multiple_of(zx(e) * 64, 64), 64)
             remote(rts.at[xq, part], ret.at[8 + xq * 4 + z], s_rtp, r_rtn.at[xq], (zx(e), at(-1, 0, 0))).start()
         remote(rts.at[1 - xq], via, s_twin, r_via, (z, aside)).start()
+
+    @pl.when(after)
+    def _():
+        work(2, kvb)
 
     hand_back(2)
     work(3, kvb)
@@ -358,6 +366,9 @@
             src = via.at[pl.ds(pl.multiple_of(zx(e) * 64, 64), 64)]
             remote(src, ret.at[8 + (1 - xq) * 4 + z], s_via, r_rtn.at[1 - xq], (zx(e), across)).start()
 
+    await_bytes(dqr, r_dq)
+    for n in range(8):
+        dq_ref[0, :, n * 512 : (n + 1) * 512] = dqr[n]
     await_bytes(ret.at[0:8], r_rt)
 
     @pl.when(last)
@@ -377,9 +388,6 @@
         dk_ref[0, :, n * 128 : (n + 1) * 128] = total[:, 0:128].astype(BF16)
         dv_ref[0, :, n * 128 : (n + 1) * 128] = total[:, 128:256].astype(BF16)
 
-    await_bytes(dqr, r_dq)
-    for n in range(8):
-        dq_ref[0, :, n * 512 : (n + 1) * 512] = dqr[n]
 
     await_bytes(qb.at[0 : 7 * 64], s_q)
     await_bytes(dob.at[0 : 7 * 64], s_do)

time: 61.6 us -> 57.9 us (0.940)
  the two profiles are of different devices: /device:TPU:30 before, /device:TPU:1 now
where the time goes in v3:
time: 57.9 us; the launch traced here: 57.7 us
  Pallas kernels  53.7 us (93%)
  local copies, waits for them, and re-layouts  3.4 us (6%)
  between operations  0.65 us (1%)
    pallas_call x1, Pallas kernels, local(): pl.pallas_call(kernel, out_shape=(jax.ShapeDtypeStruct((1, 64, 4096), BF1...  53.7 us
    unnamed x7, local copies, waits for them, and re-layouts  3.4 us

profile of v3, /device:TPU:1, one launch (start us, length us, event | category | flops | bytes accessed | tf_op | source)
XLA Modules:
  0.0 57.7 jit_solution(12682942694823109915)
XLA Ops:
  0.6 53.7 %attention_backward.1 = (bf16[1,64,4096]{2,1,0:T(8,128)(2,1)}, bf16[1,64,512]{2,1,0:T(8,128)(2,1)}, bf16[1,64,512]{2,1,0:T(8,128)(2,1)}) custom-call(bf16[1,64,4096]{2,1,0:T(8,128)(2,1)} %q_ref.1, bf16[1,64,512]{2,1,0:T(8,128)(2,1)} %k_ref.1, bf16[1,64,512]{2,1,0:T(8,128)(2,1)} %v_ref.1, bf16[1,64,4096]{2,1,0:T(8,128)(2,1)} %o_ref.1, ...), custom_call_target="tpu_custom_call" | custom-call | tf_op jit(solution)/shard_map/attention_backward/pallas_call | solution.py:438
  54.3 0.0 copy-start.1
  54.3 1.9 %copy.13 = bf16[1,64,4096]{2,1,0:T(8,128)(2,1)} copy(bf16[1,64,4096]{2,1,0:T(8,128)(2,1)} %get-tuple-element.6) | data formatting | bytes 1048576
  56.2 0.0 copy-done.1
  56.2 0.0 copy-start
  56.2 0.6 %copy.14 = bf16[1,64,512]{2,1,0:T(8,128)(2,1)} copy(bf16[1,64,512]{2,1,0:T(8,128)(2,1)S(1)} %copy-done.1) | data formatting | bytes 131072
  56.8 0.2 copy-done
  57.1 0.6 %copy.15 = bf16[1,64,512]{2,1,0:T(8,128)(2,1)} copy(bf16[1,64,512]{2,1,0:T(8,128)(2,1)S(1)} %copy-done) | data formatting | bytes 131072
Async XLA Ops:
  54.3 1.9 %copy-start.1 = (bf16[1,64,512]{2,1,0:T(8,128)(2,1)S(1)}, bf16[1,64,512]{2,1,0:T(8,128)(2,1)}, u32[]{:S(2)}) copy-start(bf16[1,64,512]{2,1,0:T(8,128)(2,1)} %get-tuple-element.7) | copy-start | bytes 196612
  56.2 0.9 %copy-start = (bf16[1,64,512]{2,1,0:T(8,128)(2,1)S(1)}, bf16[1,64,512]{2,1,0:T(8,128)(2,1)}, u32[]{:S(2)}) copy-start(bf16[1,64,512]{2,1,0:T(8,128)(2,1)} %get-tuple-element.8) | copy-start | bytes 196612

commit v4 on v3

--- a/solution.py
+++ b/solution.py
@@ -197,7 +197,7 @@
                 else:
                     pltpu.make_async_copy(src, dst, rr.at[slot]).start()
 
-    send_queries((0, 0, 0), (0, 1, 0))
+    send_queries((0, 0, 0), (0, 1, 0), (1, 0, 0), (1, 1, 0), (0, 0, 1), (0, 1, 1))
 
     @pl.when(first)
     def _():
@@ -208,7 +208,7 @@
             src = twin.at[:, pl.ds(pl.multiple_of(zx(e) % 2 * 256, 256), 256)]
             remote(src, dst, s_via, r_kva.at[theirs], (zx(e), across)).start()
 
-    send_queries((0, 0, 1), (1, 0, 0), (0, 1, 1), (1, 1, 0), (1, 0, 1), (1, 1, 1))
+    send_queries((1, 0, 1), (1, 1, 1))
     await_bytes(kvb.at[0 : 7 * 64], s_kv)
 
     for n in range(4):
@@ -431,11 +431,27 @@
         await_bytes(via, s_via)
 
 
+def settle(dq_in, dk_in, dv_in, dq_ref, dk_ref, dv_ref, dq_held, dk_held, dv_held, s_in, s_out):
+    moves = [(dk_in, dk_held, dk_ref), (dv_in, dv_held, dv_ref)]
+    for n in range(4):
+        rows = slice(n * 16, (n + 1) * 16)
+        moves.append((dq_in.at[:, rows], dq_held.at[:, rows], dq_ref.at[:, rows]))
+    came = [pltpu.make_async_copy(src, held, s_in.at[n]) for n, (src, held, _) in enumerate(moves)]
+    goes = [pltpu.make_async_copy(held, dst, s_out.at[n]) for n, (_, held, dst) in enumerate(moves)]
+    for copy in came:
+        copy.start()
+    for one, other in zip(came, goes):
+        one.wait()
+        other.start()
+    for copy in goes:
+        copy.wait()
+
+
 def local(queries, keys, values, outputs, gradient, sums, lengths):
     vmem = pl.BlockSpec(memory_space=pltpu.VMEM)
     hbm = pl.BlockSpec(memory_space=pltpu.HBM)
     dma = pltpu.SemaphoreType.DMA
-    return pl.pallas_call(
+    made = pl.pallas_call(
         kernel,
         out_shape=(
             jax.ShapeDtypeStruct((1, 64, 4096), BF16),
@@ -476,6 +492,15 @@
         ),
         name="attention_backward",
     )(queries, keys, values, outputs, gradient, jnp.transpose(sums, (0, 2, 1)), lengths)
+    return pl.pallas_call(
+        settle,
+        out_shape=tuple(jax.ShapeDtypeStruct(m.shape, m.dtype) for m in made),
+        in_specs=[hbm] * 3,
+        out_specs=(hbm,) * 3,
+        scratch_shapes=[pltpu.VMEM(m.shape, m.dtype) for m in made] + [dma((6,)), dma((6,))],
+        compiler_params=pltpu.CompilerParams(vmem_limit_bytes=63 * 2**20),
+        name="settle",
+    )(*made)
 
 
 def solution(mesh):

time: 57.9 us -> 55.6 us (0.960)
  local copies, waits for them, and re-layouts: 3.4 us -> 0 us
  Pallas kernels: 53.7 us -> 54.8 us
    unnamed x7 -> x0, local copies, waits for them, and re-layouts: 3.4 us -> none
    pallas_call x0 -> x1, Pallas kernels: none -> 1.93 us  [local(): pl.pallas_call(settle, out_shape=tuple((jax.ShapeDtypeStruct(m.shape, m.d...]
    pallas_call x1, Pallas kernels: 53.7 us -> 52.9 us  [local(): pl.pallas_call(kernel, out_shape=(jax.ShapeDtypeStruct((1, 64, 4096), BF1...]
where the time goes in v4:
time: 55.6 us; the launch traced here: 55.5 us
  Pallas kernels  54.8 us (99%)
  between operations  0.64 us (1%)
    pallas_call x1, Pallas kernels, local(): pl.pallas_call(kernel, out_shape=(jax.ShapeDtypeStruct((1, 64, 4096), BF1...  52.9 us
    pallas_call x1, Pallas kernels, local(): pl.pallas_call(settle, out_shape=tuple((jax.ShapeDtypeStruct(m.shape, m.d...  1.93 us

profile of v4, /device:TPU:1, one launch (start us, length us, event | category | flops | bytes accessed | tf_op | source)
XLA Modules:
  0.0 55.5 jit_solution(6959746001654991147)
XLA Ops:
  0.6 52.9 %attention_backward.1 = (bf16[1,64,4096]{2,1,0:T(8,128)(2,1)}, bf16[1,64,512]{2,1,0:T(8,128)(2,1)}, bf16[1,64,512]{2,1,0:T(8,128)(2,1)}) custom-call(bf16[1,64,4096]{2,1,0:T(8,128)(2,1)} %q_ref.1, bf16[1,64,512]{2,1,0:T(8,128)(2,1)} %k_ref.1, bf16[1,64,512]{2,1,0:T(8,128)(2,1)} %v_ref.1, bf16[1,64,4096]{2,1,0:T(8,128)(2,1)} %o_ref.1, ...), custom_call_target="tpu_custom_call" | custom-call | tf_op jit(solution)/shard_map/attention_backward/pallas_call | solution.py:454
  53.5 1.9 %settle.1 = (bf16[1,64,4096]{2,1,0:T(8,128)(2,1)}, bf16[1,64,512]{2,1,0:T(8,128)(2,1)}, bf16[1,64,512]{2,1,0:T(8,128)(2,1)}) custom-call(bf16[1,64,4096]{2,1,0:T(8,128)(2,1)} %get-tuple-element.6.dq_in, bf16[1,64,512]{2,1,0:T(8,128)(2,1)} %get-tuple-element.7.dk_in, bf16[1,64,512]{2,1,0:T(8,128)(2,1)} %get-tuple-element.8.dv_in), custom_call_target="tpu_custom_call" | custom-call | tf_op jit(solution)/shard_map/settle/pallas_call | solution.py:495

commit v5 on v4

--- a/solution.py
+++ b/solution.py
@@ -9,6 +9,7 @@
 F32 = jnp.float32
 BF16 = jnp.bfloat16
 SCALE = 128 ** (-0.5)
+LOG2E = 1.4426950408889634
 GROUPS = 16
 
 
@@ -245,14 +246,14 @@
     steps = lax.broadcasted_iota(jnp.int32, (256, 128), 0)
     low = lax.broadcasted_iota(jnp.int32, (8, 128), 1) < 64
 
-    def work(j, buf, count=None):
+    def work(j, buf, begin, end):
         bi = block_of(j)
         ahead = 4 if buf is kvb else 0
         lse_all = lseb[j]
         delta_all = jnp.where(low, dlb[j * 16 : j * 16 + 8], dlb[j * 16 + 8 : j * 16 + 16])
         lse_mine = jnp.where(core == 0, lse_all[0:4], lse_all[4:8])
         delta_mine = jnp.where(core == 0, delta_all[0:4], delta_all[4:8])
-        lse_row = jnp.concatenate([lse_mine[n : n + 1] for n in range(4)], axis=1)
+        lse_row = jnp.concatenate([lse_mine[n : n + 1] for n in range(4)], axis=1) * LOG2E
         delta_row = jnp.concatenate([delta_mine[n : n + 1] for n in range(4)], axis=1)
         where_open = opens[j][0:1]
         where_here = (place + 256 * bi)[0:1]
@@ -269,7 +270,7 @@
             allowed = (steps >= where_open - base) & (steps <= where_here - base)
             allowed = jnp.concatenate([allowed] * 4, axis=1)
             scores = lax.dot_general(key, qm, (((1,), (1,)), ((), ())), preferred_element_type=F32)
-            weights = jnp.where(allowed, jnp.exp(scores * SCALE - lse_row), 0.0)
+            weights = jnp.where(allowed, jnp.exp2(scores * (SCALE * LOG2E) - lse_row), 0.0)
             grads = lax.dot_general(value, dom, (((1,), (1,)), ((), ())), preferred_element_type=F32)
             shifted = (weights * (grads - delta_row) * SCALE).astype(BF16)
             acc[rows, 128:256] += jnp.dot(weights.astype(BF16), dom, preferred_element_type=F32)
@@ -277,7 +278,7 @@
             dqt[j] += lax.dot_general(key, shifted, (((0,), (0,)), ((), ())), preferred_element_type=F32)
             return 0
 
-        lax.fori_loop(0 if ahead else bi, (bi + 1 if count is None else count) if ahead else 4, lag, 0)
+        lax.fori_loop(begin, end, lag, 0)
 
     def arrived(j):
         await_bytes(lseb.at[j], r_l.at[j])
@@ -305,38 +306,44 @@
         await_bytes(pxr.at[i], r_px.at[i])
         rts[i] = (acc[blk(2 * i + core)] + pxr[i].astype(F32)).astype(BF16)
 
-    def send_back(off):
+    def send_back():
         for a in range(2):
-            i = (2 * (1 - off)) + xx(a)
             for e in range(4):
-                src = rts.at[i, pl.ds(pl.multiple_of(zx(e) * 64, 64), 64)]
-                dst = ret.at[off * 8 + xq * 4 + z]
-                if off == 0 and a == 0 and e == 0:
-                    pltpu.make_async_copy(src, dst, r_rt).start()
-                else:
-                    remote(src, dst, s_rtp if off else s_rt, r_rtn.at[xq] if off else r_rt, (zx(e), at(-off, a, 0))).start()
+                src = rts.at[xx(a), pl.ds(pl.multiple_of(zx(e) * 64, 64), 64)]
+                remote(src, ret.at[8 + xq * 4 + z], s_rtp, r_rtn.at[xq], (zx(e), at(-1, a, 0))).start()
+
+    def send_own(i):
+        for e in (2, 3, 1, 0):
+            src = rts.at[i, pl.ds(pl.multiple_of(zx(e) * 64, 64), 64)]
+            dst = ret.at[xq * 4 + z]
+            far = remote(src, dst, s_rt, r_rt, (zx(e), 4 * pair + 2 * (i - 2) + core))
+            if e:
+                far.start()
+            else:
+                pl.when(xq != i - 2)(far.start)
+                pl.when(xq == i - 2)(pltpu.make_async_copy(src, dst, r_rt).start)
 
     own_blocks()
     for j in range(2):
         arrived(j)
-        work(j, kvb)
+        work(j, kvb, 0, block_of(j) + 1)
     earlier_blocks()
     for j in range(2):
-        work(j, kva)
+        work(j, kva, block_of(j), 4)
         hand_back(j)
     for j in range(2, 4):
         arrived(j)
-        work(j, kva)
+        work(j, kva, block_of(j), 4)
     for i in range(2):
         to_partner(i)
-    pieces_left = block_of(2) + 1
-    work(2, kvb, jnp.where(after, 0, pieces_left))
+    reach = tuple(jnp.minimum(block_of(j) + 1, 2) for j in (2, 3))
+    work(2, kvb, 0, jnp.where(after, 0, reach[0]))
     for i in range(2):
         from_partner(i)
 
     @pl.when(jnp.logical_not(first | after))
     def _():
-        send_back(1)
+        send_back()
 
     @pl.when(after)
     def _():
@@ -347,17 +354,19 @@
 
     @pl.when(after)
     def _():
-        work(2, kvb)
-
+        work(2, kvb, 0, reach[0])
+
+    work(3, kvb, 0, reach[1])
+    to_partner(2)
+    work(2, kvb, 2, block_of(2) + 1)
     hand_back(2)
-    work(3, kvb)
-
-    for i in range(2, 4):
-        to_partner(i)
+    from_partner(2)
+    send_own(2)
+    work(3, kvb, 2, block_of(3) + 1)
+    to_partner(3)
     hand_back(3)
-    for i in range(2, 4):
-        from_partner(i)
-    send_back(0)
+    from_partner(3)
+    send_own(3)
 
     @pl.when(last)
     def _():

time: 55.6 us -> 54.5 us (0.980)
  Pallas kernels: 54.8 us -> 53.7 us
    pallas_call x1, Pallas kernels: 52.9 us -> 51.8 us  [local(): pl.pallas_call(kernel, out_shape=(jax.ShapeDtypeStruct((1, 64, 4096), BF1...]
where the time goes in v5:
time: 54.5 us; the launch traced here: 54.3 us
  Pallas kernels  53.7 us (99%)
  between operations  0.64 us (1%)
    pallas_call x1, Pallas kernels, local(): pl.pallas_call(kernel, out_shape=(jax.ShapeDtypeStruct((1, 64, 4096), BF1...  51.8 us
    pallas_call x1, Pallas kernels, local(): pl.pallas_call(settle, out_shape=tuple((jax.ShapeDtypeStruct(m.shape, m.d...  1.93 us

profile of v5, /device:TPU:1, one launch (start us, length us, event | category | flops | bytes accessed | tf_op | source)
XLA Modules:
  0.0 54.3 jit_solution(17223288351445262325)
XLA Ops:
  0.6 51.8 %attention_backward.1 = (bf16[1,64,4096]{2,1,0:T(8,128)(2,1)}, bf16[1,64,512]{2,1,0:T(8,128)(2,1)}, bf16[1,64,512]{2,1,0:T(8,128)(2,1)}) custom-call(bf16[1,64,4096]{2,1,0:T(8,128)(2,1)} %q_ref.1, bf16[1,64,512]{2,1,0:T(8,128)(2,1)} %k_ref.1, bf16[1,64,512]{2,1,0:T(8,128)(2,1)} %v_ref.1, bf16[1,64,4096]{2,1,0:T(8,128)(2,1)} %o_ref.1, ...), custom_call_target="tpu_custom_call" | custom-call | tf_op jit(solution)/shard_map/attention_backward/pallas_call | solution.py:463
  52.4 1.9 %settle.1 = (bf16[1,64,4096]{2,1,0:T(8,128)(2,1)}, bf16[1,64,512]{2,1,0:T(8,128)(2,1)}, bf16[1,64,512]{2,1,0:T(8,128)(2,1)}) custom-call(bf16[1,64,4096]{2,1,0:T(8,128)(2,1)} %get-tuple-element.6.dq_in, bf16[1,64,512]{2,1,0:T(8,128)(2,1)} %get-tuple-element.7.dk_in, bf16[1,64,512]{2,1,0:T(8,128)(2,1)} %get-tuple-element.8.dv_in), custom_call_target="tpu_custom_call" | custom-call | tf_op jit(solution)/shard_map/settle/pallas_call | solution.py:504

commit v6 on v5

--- a/solution.py
+++ b/solution.py
@@ -60,7 +60,7 @@
     for a in range(2):
         for b in range(2):
             for e in range(4):
-                if a or b or e:
+                if (a or b or e) and not (b and e == 3):
                     pl.semaphore_signal(barrier, inc=1, device_id=(zx(e), at(0, a, b)), device_id_type=MESH)
 
     @pl.when(jnp.logical_not(first))
@@ -114,6 +114,36 @@
     for n in range(4):
         kvs[:, n * 256 : n * 256 + 128] = kin[0, :, n * 128 : (n + 1) * 128]
         kvs[:, n * 256 + 128 : (n + 1) * 256] = kin[1, :, n * 128 : (n + 1) * 128]
+
+    pl.semaphore_wait(barrier, 13 + 8 * ((pair + GROUPS - 1) // GROUPS) + 8 * ((2 * GROUPS - 2 - pair) // GROUPS) + jnp.where(bridge, 5, 0))
+
+    rows_own = pl.ds(pl.multiple_of(own * 256 + z * 64, 64), 64)
+
+    def send_kv(off, a, e):
+        there = 2 * xx(a) + zx(e) % 2
+        src = kvs.at[:, pl.ds(pl.multiple_of(there * 256, 256), 256)]
+        if off:
+            remote(src, kva.at[rows_own], s_kvn, r_kva.at[own], (zx(e), at(1, a, 0))).start()
+        elif a or e:
+            remote(src, kvb.at[rows_own], s_kv, r_kvb.at[own], (zx(e), at(0, a, 0))).start()
+        else:
+            pltpu.make_async_copy(src, kvb.at[rows_own], r_kvb.at[own]).start()
+
+    @pl.when(before)
+    def _():
+        for e in range(4):
+            src = kvs.at[:, pl.ds(pl.multiple_of((2 * xq + zx(e) % 2) * 256, 256), 256)]
+            remote(src, kva.at[rows_own], s_kvn, r_kva.at[own], (zx(e), at(1, 0, 0))).start()
+        src = kvs.at[:, pl.ds(pl.multiple_of((1 - xq) * 512, 512), 512)]
+        remote(src, twin, s_twin, r_twin, (z, aside)).start()
+
+    for a, e in ((0, 0), (0, 2), (1, 0), (0, 3), (1, 2), (0, 1), (1, 3), (1, 1)):
+        send_kv(0, a, e)
+
+    @pl.when(jnp.logical_not(last | before))
+    def _():
+        for a, e in ((0, 2), (1, 2), (0, 3), (1, 3), (0, 0), (0, 1), (1, 0), (1, 1)):
+            send_kv(1, a, e)
 
     for load in loads[2:]:
         load.wait()
@@ -125,36 +155,6 @@
     both = jnp.concatenate([delta, delta], axis=0).T
     for n in range(4):
         dls[n] = both[n * 8 : (n + 1) * 8]
-
-    pl.semaphore_wait(barrier, 15 + 8 * ((pair + GROUPS - 1) // GROUPS) + 8 * ((2 * GROUPS - 2 - pair) // GROUPS) + jnp.where(bridge, 5, 0))
-
-    rows_own = pl.ds(pl.multiple_of(own * 256 + z * 64, 64), 64)
-
-    def send_kv(off, a, e):
-        there = 2 * xx(a) + zx(e) % 2
-        src = kvs.at[:, pl.ds(pl.multiple_of(there * 256, 256), 256)]
-        if off:
-            remote(src, kva.at[rows_own], s_kvn, r_kva.at[own], (zx(e), at(1, a, 0))).start()
-        elif a or e:
-            remote(src, kvb.at[rows_own], s_kv, r_kvb.at[own], (zx(e), at(0, a, 0))).start()
-        else:
-            pltpu.make_async_copy(src, kvb.at[rows_own], r_kvb.at[own]).start()
-
-    @pl.when(before)
-    def _():
-        for e in range(4):
-            src = kvs.at[:, pl.ds(pl.multiple_of((2 * xq + zx(e) % 2) * 256, 256), 256)]
-            remote(src, kva.at[rows_own], s_kvn, r_kva.at[own], (zx(e), at(1, 0, 0))).start()
-        src = kvs.at[:, pl.ds(pl.multiple_of((1 - xq) * 512, 512), 512)]
-        remote(src, twin, s_twin, r_twin, (z, aside)).start()
-
-    for a, e in ((0, 0), (0, 2), (1, 0), (0, 3), (1, 2), (0, 1), (1, 3), (1, 1)):
-        send_kv(0, a, e)
-
-    @pl.when(jnp.logical_not(last | before))
-    def _():
-        for a, e in ((0, 2), (1, 2), (0, 3), (1, 3), (0, 0), (0, 1), (1, 0), (1, 1)):
-            send_kv(1, a, e)
 
     to_x = z // 2
     for e in (0, 2):
@@ -324,16 +324,18 @@
                 pl.when(xq == i - 2)(pltpu.make_async_copy(src, dst, r_rt).start)
 
     own_blocks()
-    for j in range(2):
-        arrived(j)
-        work(j, kvb, 0, block_of(j) + 1)
+    arrived(0)
+    work(0, kvb, 0, block_of(0) + 1)
     earlier_blocks()
-    for j in range(2):
-        work(j, kva, block_of(j), 4)
-        hand_back(j)
+    work(0, kva, jnp.where(first, 4, block_of(0)), 4)
+    hand_back(0)
+    arrived(1)
+    work(1, kvb, 0, block_of(1) + 1)
+    work(1, kva, jnp.where(first, 4, block_of(1)), 4)
+    hand_back(1)
     for j in range(2, 4):
         arrived(j)
-        work(j, kva, block_of(j), 4)
+        work(j, kva, jnp.where(first, 4, block_of(j)), 4)
     for i in range(2):
         to_partner(i)
     reach = tuple(jnp.minimum(block_of(j) + 1, 2) for j in (2, 3))

time: 54.5 us -> 54.4 us (level); the launches traced: 54.3 us -> 53.5 us
  Pallas kernels: 53.7 us -> 52.8 us
    pallas_call x1, Pallas kernels: 51.8 us -> 50.9 us  [local(): pl.pallas_call(kernel, out_shape=(jax.ShapeDtypeStruct((1, 64, 4096), BF1...]
where the time goes in v6:
time: 54.4 us; the launch traced here: 53.5 us
  Pallas kernels  52.8 us (97%)
  between operations  0.64 us (1%)
    pallas_call x1, Pallas kernels, local(): pl.pallas_call(kernel, out_shape=(jax.ShapeDtypeStruct((1, 64, 4096), BF1...  50.9 us
    pallas_call x1, Pallas kernels, local(): pl.pallas_call(settle, out_shape=tuple((jax.ShapeDtypeStruct(m.shape, m.d...  1.93 us

profile of v6, /device:TPU:1, one launch (start us, length us, event | category | flops | bytes accessed | tf_op | source)
XLA Modules:
  0.0 53.5 jit_solution(7476751770242034301)
XLA Ops:
  0.6 50.9 %attention_backward.1 = (bf16[1,64,4096]{2,1,0:T(8,128)(2,1)}, bf16[1,64,512]{2,1,0:T(8,128)(2,1)}, bf16[1,64,512]{2,1,0:T(8,128)(2,1)}) custom-call(bf16[1,64,4096]{2,1,0:T(8,128)(2,1)} %q_ref.1, bf16[1,64,512]{2,1,0:T(8,128)(2,1)} %k_ref.1, bf16[1,64,512]{2,1,0:T(8,128)(2,1)} %v_ref.1, bf16[1,64,4096]{2,1,0:T(8,128)(2,1)} %o_ref.1, ...), custom_call_target="tpu_custom_call" | custom-call | tf_op jit(solution)/shard_map/attention_backward/pallas_call | solution.py:465
  51.6 1.9 %settle.1 = (bf16[1,64,4096]{2,1,0:T(8,128)(2,1)}, bf16[1,64,512]{2,1,0:T(8,128)(2,1)}, bf16[1,64,512]{2,1,0:T(8,128)(2,1)}) custom-call(bf16[1,64,4096]{2,1,0:T(8,128)(2,1)} %get-tuple-element.6.dq_in, bf16[1,64,512]{2,1,0:T(8,128)(2,1)} %get-tuple-element.7.dk_in, bf16[1,64,512]{2,1,0:T(8,128)(2,1)} %get-tuple-element.8.dv_in), custom_call_target="tpu_custom_call" | custom-call | tf_op jit(solution)/shard_map/settle/pallas_call | solution.py:506

commit v7 on v6

--- a/solution.py
+++ b/solution.py
@@ -443,10 +443,11 @@
 
 
 def settle(dq_in, dk_in, dv_in, dq_ref, dk_ref, dv_ref, dq_held, dk_held, dv_held, s_in, s_out):
-    moves = [(dk_in, dk_held, dk_ref), (dv_in, dv_held, dv_ref)]
-    for n in range(4):
-        rows = slice(n * 16, (n + 1) * 16)
+    moves = []
+    for n in range(2):
+        rows = slice(n * 32, (n + 1) * 32)
         moves.append((dq_in.at[:, rows], dq_held.at[:, rows], dq_ref.at[:, rows]))
+    moves += [(dk_in, dk_held, dk_ref), (dv_in, dv_held, dv_ref)]
     came = [pltpu.make_async_copy(src, held, s_in.at[n]) for n, (src, held, _) in enumerate(moves)]
     goes = [pltpu.make_async_copy(held, dst, s_out.at[n]) for n, (_, held, dst) in enumerate(moves)]
     for copy in came:
@@ -508,7 +509,7 @@
         out_shape=tuple(jax.ShapeDtypeStruct(m.shape, m.dtype) for m in made),
         in_specs=[hbm] * 3,
         out_specs=(hbm,) * 3,
-        scratch_shapes=[pltpu.VMEM(m.shape, m.dtype) for m in made] + [dma((6,)), dma((6,))],
+        scratch_shapes=[pltpu.VMEM(m.shape, m.dtype) for m in made] + [dma((4,)), dma((4,))],
         compiler_params=pltpu.CompilerParams(vmem_limit_bytes=63 * 2**20),
         name="settle",
     )(*made)

time: 54.4 us -> 54.3 us (level)
  no operation moved by 1% of the time
where the time goes in v7:
time: 54.3 us; the launch traced here: 53.4 us
  Pallas kernels  52.8 us (97%)
  between operations  0.64 us (1%)
    pallas_call x1, Pallas kernels, local(): pl.pallas_call(kernel, out_shape=(jax.ShapeDtypeStruct((1, 64, 4096), BF1...  50.9 us
    pallas_call x1, Pallas kernels, local(): pl.pallas_call(settle, out_shape=tuple((jax.ShapeDtypeStruct(m.shape, m.d...  1.84 us

profile of v7, /device:TPU:1, one launch (start us, length us, event | category | flops | bytes accessed | tf_op | source)
XLA Modules:
  0.0 53.4 jit_solution(10833794290195744492)
XLA Ops:
  0.6 50.9 %attention_backward.1 = (bf16[1,64,4096]{2,1,0:T(8,128)(2,1)}, bf16[1,64,512]{2,1,0:T(8,128)(2,1)}, bf16[1,64,512]{2,1,0:T(8,128)(2,1)}) custom-call(bf16[1,64,4096]{2,1,0:T(8,128)(2,1)} %q_ref.1, bf16[1,64,512]{2,1,0:T(8,128)(2,1)} %k_ref.1, bf16[1,64,512]{2,1,0:T(8,128)(2,1)} %v_ref.1, bf16[1,64,4096]{2,1,0:T(8,128)(2,1)} %o_ref.1, ...), custom_call_target="tpu_custom_call" | custom-call | tf_op jit(solution)/shard_map/attention_backward/pallas_call | solution.py:466
  51.6 1.8 %settle.1 = (bf16[1,64,4096]{2,1,0:T(8,128)(2,1)}, bf16[1,64,512]{2,1,0:T(8,128)(2,1)}, bf16[1,64,512]{2,1,0:T(8,128)(2,1)}) custom-call(bf16[1,64,4096]{2,1,0:T(8,128)(2,1)} %get-tuple-element.6.dq_in, bf16[1,64,512]{2,1,0:T(8,128)(2,1)} %get-tuple-element.7.dk_in, bf16[1,64,512]{2,1,0:T(8,128)(2,1)} %get-tuple-element.8.dv_in), custom_call_target="tpu_custom_call" | custom-call | tf_op jit(solution)/shard_map/settle/pallas_call | solution.py:507
